TPU v7x, 32 devices: a whole 2x2x4 slice. The times are simulated.
32 devices in a mesh: dp: 4 (over z), fsdp: 8 (over y, x, core).
Axes of the slice: x: 2, y: 2, z: 4, core: 2. Of those that a mesh axis runs over, the one named last changes fastest.
Arguments:
- inputs: float32 [32768, 768], P(('dp', 'fsdp')), may hold values from -6 to 6
- lengths: int32 [64], P(('dp', 'fsdp')), may hold values from 1 to 512, as said below
- query_weight: bfloat16 [768, 768], P(('dp', 'fsdp')), may hold values from -0.21875 to 0.21875
- key_weight: bfloat16 [768, 768], P(('dp', 'fsdp')), may hold values from -0.21875 to 0.21875
- value_weight: bfloat16 [768, 768], P(('dp', 'fsdp')), may hold values from -0.21875 to 0.21875
- out_weight: bfloat16 [768, 768], P(('dp', 'fsdp')), may hold values from -1.75 to 1.75
- query_bias: bfloat16 [768], P(('dp', 'fsdp')), may hold values from -1.5 to 1.5
- value_bias: bfloat16 [768], P(('dp', 'fsdp')), may hold values from -1.5 to 1.5
- out_bias: bfloat16 [768], P(('dp', 'fsdp')), may hold values from -1.5 to 1.5
- first_gain: bfloat16 [768], P(('dp', 'fsdp')), may hold values from 0.5 to 1.5
- first_shift: bfloat16 [768], P(('dp', 'fsdp')), may hold values from -1.5 to 1.5
- inner_weight: bfloat16 [768, 3072], P(('dp', 'fsdp')), may hold values from -0.21875 to 0.21875
- inner_bias: bfloat16 [3072], P(('dp', 'fsdp')), may hold values from -1.5 to 1.5
- down_weight: bfloat16 [3072, 768], P(('dp', 'fsdp')), may hold values from -0.109375 to 0.109375
- down_bias: bfloat16 [768], P(('dp', 'fsdp')), may hold values from -1.5 to 1.5
- second_gain: bfloat16 [768], P(('dp', 'fsdp')), may hold values from 0.5 to 1.5
- second_shift: bfloat16 [768], P(('dp', 'fsdp')), may hold values from -1.5 to 1.5
- cotangent: float32 [32768, 768], P(('dp', 'fsdp')), may hold values from -6 to 6
Outputs:
- output: float32 [32768, 768], P(('dp', 'fsdp'))
- grad_input: float32 [32768, 768], P(('dp', 'fsdp'))
- grad_query_weight: float32 [768, 768], P(('dp', 'fsdp'))
- grad_key_weight: float32 [768, 768], P(('dp', 'fsdp'))
- grad_value_weight: float32 [768, 768], P(('dp', 'fsdp'))
- grad_out_weight: float32 [768, 768], P(('dp', 'fsdp'))
- grad_query_bias: float32 [768], P(('dp', 'fsdp'))
- grad_value_bias: float32 [768], P(('dp', 'fsdp'))
- grad_out_bias: float32 [768], P(('dp', 'fsdp'))
- grad_first_gain: float32 [768], P(('dp', 'fsdp'))
- grad_first_shift: float32 [768], P(('dp', 'fsdp'))
- grad_inner_weight: float32 [768, 3072], P(('dp', 'fsdp'))
- grad_inner_bias: float32 [3072], P(('dp', 'fsdp'))
- grad_down_weight: float32 [3072, 768], P(('dp', 'fsdp'))
- grad_down_bias: float32 [768], P(('dp', 'fsdp'))
- grad_second_gain: float32 [768], P(('dp', 'fsdp'))
- grad_second_shift: float32 [768], P(('dp', 'fsdp'))
Inputs may be any that keep to these rules, and one draw needn't show every extreme that they name: `lengths`: positions of a pair below its entry are tokens, the rest padding; some pair has all 512 positions valid.
All inputs are finite; a program needn't handle non-finite values.
Results may differ from a plain program's by a relative error of at most 0.014.
The roundings to bfloat16 on the way count: a program that leaves them out, or rounds other values in their place, can miss the bound.
Values may be sent and summed in bfloat16 or wider, within the bound.
No kernel may reach another device: no remote copies, remote signals or barrier semaphores. Data moves between devices by JAX's collectives and lax.ppermute only.
A program may use at most 192 MiB of HBM per device.

v0:
```python
import jax
import jax.numpy as jnp
from jax import lax
from jax.sharding import PartitionSpec as P

H = 12
DH = 64


NORM_EPSILON = 1e-12
MASKED_SCORE = -1000000000.0
ROOT_HALF = 0.7071067811865476
GAUSS_DENSITY = 0.3989422804014327


def product(lhs_rows, rhs_cols):
    return jnp.dot(lhs_rows, rhs_cols, preferred_element_type=jnp.float32)


def left_product(lhs_rows, rhs_cols):
    return lax.dot_general(
        lhs_rows, rhs_cols, (((0,), (0,)), ((), ())), preferred_element_type=jnp.float32
    )


def right_product(lhs_rows, rhs_cols):
    return lax.dot_general(
        lhs_rows, rhs_cols, (((1,), (1,)), ((), ())), preferred_element_type=jnp.float32
    )


def norm_rows(total_in, norm_gain, norm_shift):
    center = total_in - jnp.mean(total_in, axis=-1, keepdims=True)
    norm_scale = lax.rsqrt(jnp.mean(center * center, axis=-1, keepdims=True) + NORM_EPSILON)
    normed = center * norm_scale
    return (normed * norm_gain + norm_shift, normed, norm_scale)


def norm_back(upstream, normed, norm_scale, norm_gain):
    scaled = upstream * norm_gain
    return norm_scale * (
        scaled
        - jnp.mean(scaled, axis=-1, keepdims=True)
        - normed * jnp.mean(scaled * normed, axis=-1, keepdims=True)
    )


def masked_scores(queries, key_rows, length):
    scores = (
        jnp.einsum("qhe,khe->hqk", queries, key_rows, preferred_element_type=jnp.float32) * 0.125
    )
    visible = (jnp.arange(queries.shape[0]) < length)[None, None, :]
    return jnp.where(visible, scores, MASKED_SCORE)


def attend_forward(packed):
    queries, key_rows, value_rows, length = packed
    scores = masked_scores(queries, key_rows, length)
    row_peak = jnp.max(scores, axis=-1, keepdims=True)
    exponent = jnp.exp(scores - row_peak)
    exp_total = jnp.sum(exponent, axis=-1, keepdims=True)
    attention = (exponent / exp_total).astype(jnp.bfloat16)
    attended = jnp.einsum("hqk,khe->qhe", attention, value_rows, preferred_element_type=jnp.float32)
    return (attended.astype(jnp.bfloat16), row_peak + jnp.log(exp_total))


def attend_backward(packed):
    queries, key_rows, value_rows, upstream, log_total, length = packed
    attention = jnp.exp(masked_scores(queries, key_rows, length) - log_total)
    attention_low = attention.astype(jnp.bfloat16)
    value_back = jnp.einsum(
        "hqk,qhe->khe", attention_low, upstream, preferred_element_type=jnp.float32
    )
    weight_back = jnp.einsum(
        "qhe,khe->hqk", upstream, value_rows, preferred_element_type=jnp.float32
    )
    score_back = (
        attention * (weight_back - jnp.sum(weight_back * attention, axis=-1, keepdims=True))
    ).astype(jnp.bfloat16)
    query_back = (
        jnp.einsum("hqk,khe->qhe", score_back, key_rows, preferred_element_type=jnp.float32) * 0.125
    )
    key_back = (
        jnp.einsum("hqk,qhe->khe", score_back, queries, preferred_element_type=jnp.float32) * 0.125
    )
    return (
        query_back.astype(jnp.bfloat16),
        key_back.astype(jnp.bfloat16),
        value_back.astype(jnp.bfloat16),
    )


def gather_first(params):
    (
        query_weight,
        key_weight,
        value_weight,
        out_weight,
        query_bias,
        value_bias,
        out_bias,
        first_gain,
        first_shift,
        inner_weight,
        inner_bias,
        down_weight,
        down_bias,
        second_gain,
        second_shift,
    ) = params
    return (
        lax.all_gather(query_weight, ("dp", "fsdp"), axis=0, tiled=True),
        lax.all_gather(key_weight, ("dp", "fsdp"), axis=0, tiled=True),
        lax.all_gather(value_weight, ("dp", "fsdp"), axis=0, tiled=True),
        lax.all_gather(out_weight, ("dp", "fsdp"), axis=0, tiled=True),
        lax.all_gather(query_bias, ("dp", "fsdp"), axis=0, tiled=True),
        lax.all_gather(value_bias, ("dp", "fsdp"), axis=0, tiled=True),
        lax.all_gather(out_bias, ("dp", "fsdp"), axis=0, tiled=True),
        lax.all_gather(first_gain, ("dp", "fsdp"), axis=0, tiled=True),
        lax.all_gather(first_shift, ("dp", "fsdp"), axis=0, tiled=True),
        lax.all_gather(inner_weight, ("dp", "fsdp"), axis=0, tiled=True),
        lax.all_gather(inner_bias, ("dp", "fsdp"), axis=0, tiled=True),
        lax.all_gather(down_weight, ("dp", "fsdp"), axis=0, tiled=True),
        lax.all_gather(down_bias, ("dp", "fsdp"), axis=0, tiled=True),
        lax.all_gather(second_gain, ("dp", "fsdp"), axis=0, tiled=True),
        lax.all_gather(second_shift, ("dp", "fsdp"), axis=0, tiled=True),
    )


def gather_again(params):
    (
        query_weight,
        key_weight,
        value_weight,
        out_weight,
        query_bias,
        value_bias,
        out_bias,
        first_gain,
        first_shift,
        inner_weight,
        inner_bias,
        down_weight,
        down_bias,
        second_gain,
        second_shift,
    ) = params
    return (
        lax.all_gather(query_weight, ("dp", "fsdp"), axis=0, tiled=True),
        lax.all_gather(key_weight, ("dp", "fsdp"), axis=0, tiled=True),
        lax.all_gather(value_weight, ("dp", "fsdp"), axis=0, tiled=True),
        lax.all_gather(out_weight, ("dp", "fsdp"), axis=0, tiled=True),
        lax.all_gather(query_bias, ("dp", "fsdp"), axis=0, tiled=True),
        lax.all_gather(value_bias, ("dp", "fsdp"), axis=0, tiled=True),
        lax.all_gather(out_bias, ("dp", "fsdp"), axis=0, tiled=True),
        lax.all_gather(first_gain, ("dp", "fsdp"), axis=0, tiled=True),
        lax.all_gather(first_shift, ("dp", "fsdp"), axis=0, tiled=True),
        lax.all_gather(inner_weight, ("dp", "fsdp"), axis=0, tiled=True),
        lax.all_gather(inner_bias, ("dp", "fsdp"), axis=0, tiled=True),
        lax.all_gather(down_weight, ("dp", "fsdp"), axis=0, tiled=True),
        lax.all_gather(down_bias, ("dp", "fsdp"), axis=0, tiled=True),
        lax.all_gather(second_gain, ("dp", "fsdp"), axis=0, tiled=True),
        lax.all_gather(second_shift, ("dp", "fsdp"), axis=0, tiled=True),
    )


def settle_grads(gradients):
    (
        query_weight,
        key_weight,
        value_weight,
        out_weight,
        query_bias,
        value_bias,
        out_bias,
        first_gain,
        first_shift,
        inner_weight,
        inner_bias,
        down_weight,
        down_bias,
        second_gain,
        second_shift,
    ) = gradients
    return (
        lax.psum_scatter(query_weight, ("dp", "fsdp"), scatter_dimension=0, tiled=True),
        lax.psum_scatter(key_weight, ("dp", "fsdp"), scatter_dimension=0, tiled=True),
        lax.psum_scatter(value_weight, ("dp", "fsdp"), scatter_dimension=0, tiled=True),
        lax.psum_scatter(out_weight, ("dp", "fsdp"), scatter_dimension=0, tiled=True),
        lax.psum_scatter(query_bias, ("dp", "fsdp"), scatter_dimension=0, tiled=True),
        lax.psum_scatter(value_bias, ("dp", "fsdp"), scatter_dimension=0, tiled=True),
        lax.psum_scatter(out_bias, ("dp", "fsdp"), scatter_dimension=0, tiled=True),
        lax.psum_scatter(first_gain, ("dp", "fsdp"), scatter_dimension=0, tiled=True),
        lax.psum_scatter(first_shift, ("dp", "fsdp"), scatter_dimension=0, tiled=True),
        lax.psum_scatter(inner_weight, ("dp", "fsdp"), scatter_dimension=0, tiled=True),
        lax.psum_scatter(inner_bias, ("dp", "fsdp"), scatter_dimension=0, tiled=True),
        lax.psum_scatter(down_weight, ("dp", "fsdp"), scatter_dimension=0, tiled=True),
        lax.psum_scatter(down_bias, ("dp", "fsdp"), scatter_dimension=0, tiled=True),
        lax.psum_scatter(second_gain, ("dp", "fsdp"), scatter_dimension=0, tiled=True),
        lax.psum_scatter(second_shift, ("dp", "fsdp"), scatter_dimension=0, tiled=True),
    )


def local(
    inputs,
    lengths,
    query_weight,
    key_weight,
    value_weight,
    out_weight,
    query_bias,
    value_bias,
    out_bias,
    first_gain,
    first_shift,
    inner_weight,
    inner_bias,
    down_weight,
    down_bias,
    second_gain,
    second_shift,
    cotangent,
):
    shards = (
        query_weight,
        key_weight,
        value_weight,
        out_weight,
        query_bias,
        value_bias,
        out_bias,
        first_gain,
        first_shift,
        inner_weight,
        inner_bias,
        down_weight,
        down_bias,
        second_gain,
        second_shift,
    )
    (
        query_weight,
        key_weight,
        value_weight,
        out_weight,
        query_bias,
        value_bias,
        out_bias,
        first_gain,
        first_shift,
        inner_weight,
        inner_bias,
        down_weight,
        down_bias,
        second_gain,
        second_shift,
    ) = gather_first(shards)
    row_count, feature_count = inputs.shape
    seq_count = lengths.shape[0]
    positions = row_count // seq_count
    head_shape = (seq_count, positions, H, DH)
    lowered = inputs.astype(jnp.bfloat16)
    queries = (product(lowered, query_weight) + query_bias.astype(jnp.float32)).astype(jnp.bfloat16)
    key_rows = product(lowered, key_weight).astype(jnp.bfloat16)
    value_rows = (product(lowered, value_weight) + value_bias.astype(jnp.float32)).astype(
        jnp.bfloat16
    )
    attended, log_total = lax.map(
        attend_forward,
        (
            queries.reshape(head_shape),
            key_rows.reshape(head_shape),
            value_rows.reshape(head_shape),
            lengths,
        ),
    )
    attended_rows = attended.reshape(row_count, feature_count)
    first_sum = inputs + product(attended_rows, out_weight) + out_bias.astype(jnp.float32)
    first_scale_gain = first_gain.astype(jnp.float32)
    hidden, first_normed, first_rstd = norm_rows(
        first_sum, first_scale_gain, first_shift.astype(jnp.float32)
    )
    hidden_low = hidden.astype(jnp.bfloat16)
    inner_sum = product(hidden_low, inner_weight) + inner_bias.astype(jnp.float32)
    active = jax.nn.gelu(inner_sum, approximate=False).astype(jnp.bfloat16)
    second_sum = hidden + product(active, down_weight) + down_bias.astype(jnp.float32)
    second_scale_gain = second_gain.astype(jnp.float32)
    output, second_normed, second_rstd = norm_rows(
        second_sum, second_scale_gain, second_shift.astype(jnp.float32)
    )
    back_params = gather_again(shards)
    (
        query_weight,
        key_weight,
        value_weight,
        out_weight,
        query_bias,
        value_bias,
        out_bias,
        first_gain,
        first_shift,
        inner_weight,
        inner_bias,
        down_weight,
        down_bias,
        second_gain,
        second_shift,
    ) = back_params
    grad_second_gain = jnp.sum(cotangent * second_normed, axis=0)
    grad_second_shift = jnp.sum(cotangent, axis=0)
    second_back = norm_back(cotangent, second_normed, second_rstd, second_scale_gain)
    down_back = second_back.astype(jnp.bfloat16)
    grad_down_bias = jnp.sum(down_back.astype(jnp.float32), axis=0)
    grad_down_weight = left_product(active, down_back)
    gelu_slope = (
        0.5 * (1.0 + lax.erf(inner_sum * ROOT_HALF))
        + inner_sum * jnp.exp(-0.5 * inner_sum * inner_sum) * GAUSS_DENSITY
    )
    inner_back = (right_product(down_back, down_weight) * gelu_slope).astype(jnp.bfloat16)
    grad_inner_bias = jnp.sum(inner_back.astype(jnp.float32), axis=0)
    grad_inner_weight = left_product(hidden_low, inner_back)
    hidden_back = second_back + right_product(inner_back, inner_weight)
    grad_first_gain = jnp.sum(hidden_back * first_normed, axis=0)
    grad_first_shift = jnp.sum(hidden_back, axis=0)
    first_back = norm_back(hidden_back, first_normed, first_rstd, first_scale_gain)
    branch_back = first_back.astype(jnp.bfloat16)
    grad_out_bias = jnp.sum(branch_back.astype(jnp.float32), axis=0)
    grad_out_weight = left_product(attended_rows, branch_back)
    attended_back = right_product(branch_back, out_weight).astype(jnp.bfloat16)
    query_back, key_back, value_back = lax.map(
        attend_backward,
        (
            queries.reshape(head_shape),
            key_rows.reshape(head_shape),
            value_rows.reshape(head_shape),
            attended_back.reshape(head_shape),
            log_total,
            lengths,
        ),
    )
    query_back = query_back.reshape(row_count, feature_count)
    key_back = key_back.reshape(row_count, feature_count)
    value_back = value_back.reshape(row_count, feature_count)
    grad_query_weight = left_product(lowered, query_back)
    grad_key_weight = left_product(lowered, key_back)
    grad_value_weight = left_product(lowered, value_back)
    grad_query_bias = jnp.sum(query_back.astype(jnp.float32), axis=0)
    grad_value_bias = jnp.sum(value_back.astype(jnp.float32), axis=0)
    grad_input = (
        first_back
        + right_product(query_back, query_weight)
        + right_product(key_back, key_weight)
        + right_product(value_back, value_weight)
    )
    settled = settle_grads(
        (
            grad_query_weight,
            grad_key_weight,
            grad_value_weight,
            grad_out_weight,
            grad_query_bias,
            grad_value_bias,
            grad_out_bias,
            grad_first_gain,
            grad_first_shift,
            grad_inner_weight,
            grad_inner_bias,
            grad_down_weight,
            grad_down_bias,
            grad_second_gain,
            grad_second_shift,
        )
    )
    return (output, grad_input) + tuple(settled)


def solution(mesh):
    return jax.shard_map(
        local,
        mesh=mesh,
        in_specs=(
            P(("dp", "fsdp"), None),
            P(("dp", "fsdp")),
            P(("dp", "fsdp"), None),
            P(("dp", "fsdp"), None),
            P(("dp", "fsdp"), None),
            P(("dp", "fsdp"), None),
            P(("dp", "fsdp")),
            P(("dp", "fsdp")),
            P(("dp", "fsdp")),
            P(("dp", "fsdp")),
            P(("dp", "fsdp")),
            P(("dp", "fsdp"), None),
            P(("dp", "fsdp")),
            P(("dp", "fsdp"), None),
            P(("dp", "fsdp")),
            P(("dp", "fsdp")),
            P(("dp", "fsdp")),
            P(("dp", "fsdp"), None),
        ),
        out_specs=(
            P(("dp", "fsdp"), None),
            P(("dp", "fsdp"), None),
            P(("dp", "fsdp"), None),
            P(("dp", "fsdp"), None),
            P(("dp", "fsdp"), None),
            P(("dp", "fsdp"), None),
            P(("dp", "fsdp")),
            P(("dp", "fsdp")),
            P(("dp", "fsdp")),
            P(("dp", "fsdp")),
            P(("dp", "fsdp")),
            P(("dp", "fsdp"), None),
            P(("dp", "fsdp")),
            P(("dp", "fsdp"), None),
            P(("dp", "fsdp")),
            P(("dp", "fsdp")),
            P(("dp", "fsdp")),
        ),
        check_vma=False,
    )
```

profile of v0, /device:TPU:0, one launch (start us, length us, event | category | flops | bytes accessed | tf_op | source)
XLA Modules:
  0.0 1117.1 jit_solution(13210511250848725910)
XLA Ops:
  19.0 42.4 %all-reduce.19 = (bf16[768]{0:T(1024)(128)(2,1)S(1)}, bf16[768]{0:T(1024)(128)(2,1)S(1)}, bf16[768]{0:T(1024)(128)(2,1)S(1)}, bf16[768]{0:T(1024)(128)(2,1)S(1)}...) all-reduce(bf16[768]{0:T(1024)(128)(2,1)S(1)} %dynamic-update-slice, ...), channel_id=1, replica_groups=mesh['dp'=4,'fsdp'=8] {'dp','fsdp'}, use_global_device_ids=true, to_apply=%add | all-reduce | flops 9216 | bytes 36864
  74.1 49.9 %all-gather.9.cloned.1.call-done = bf16[768,768]{1,0:T(8,128)(2,1)} async-done(((bf16[24,768]{1,0:T(8,128)(2,1)}), bf16[768,768]{1,0:T(8,128)(2,1)}) %all-gather.9.cloned.1.call-update) | async-done | bytes 1179664 | tf_op jit(solution)/shard_map/all_gather | solution.py:112
  128.9 50.9 %all-gather.11.cloned.1.call-done = bf16[768,768]{1,0:T(8,128)(2,1)} async-done(((bf16[24,768]{1,0:T(8,128)(2,1)}), bf16[768,768]{1,0:T(8,128)(2,1)}) %all-gather.11.cloned.1.call-update) | async-done | bytes 1179664 | tf_op jit(solution)/shard_map/all_gather | solution.py:113
  179.9 4.3 convolution_convert_fusion.1
  191.4 22.6 %while.26 = (s32[]{:T(128)}, bf16[2,512,12,64]{1,3,2,0:T(8,128)(2,1)}, f32[2,12,512,1]{2,1,3,0:T(8,128)S(1)}, bf16[2,512,12,64]{1,3,2,0:T(8,128)(2,1)}, s32[2]{0...) while((s32[]{:T(128)}, ...), condition=%wide.region_3.4_spmd, body=%wide.region_0.3_spmd.sunk | while | flops 843442688 | bytes 47427716 | solution.py:268
  198.6 4.2 fusion.139
  209.8 4.2 fusion.139
  214.0 4.2 copy.101
  219.7 15.9 %all-gather.13.cloned.1.call-done = bf16[768,768]{1,0:T(8,128)(2,1)} async-done(((bf16[24,768]{1,0:T(8,128)(2,1)}), bf16[768,768]{1,0:T(8,128)(2,1)}) %all-gather.13.cloned.1.call-update) | async-done | bytes 1179664 | tf_op jit(solution)/shard_map/all_gather | solution.py:115
  235.7 4.2 fusion.84
  240.3 60.7 %all-gather.15.cloned.1.call-done = bf16[768,3072]{1,0:T(8,128)(2,1)} async-done(((bf16[24,3072]{1,0:T(8,128)(2,1)}), bf16[768,3072]{1,0:T(8,128)(2,1)}) %all-gather.15.cloned.1.call-update) | async-done | bytes 4718608 | tf_op jit(solution)/shard_map/all_gather | solution.py:121
  301.0 49.4 %fusion.59 = (bf16[1024,3072]{1,0:T(8,128)(2,1)}, f32[1024,3072]{1,0:T(8,128)}) fusion(f32[3072]{0:T(1024)S(1)} %convert_element_type.117, bf16[768,3072]{1,0:T(8,128)(2,1)} %all-gather.15.cloned.1.call-done, f32[1024,768]{0,1:T(8,128)S(1)} %get-tuple-element.285, f32[768]{0:T(1024)S(1)} %convert_element_type.115, f32[768]{0:T(1024)S(1)} %convert_element_type.114, ...), kind=kOutput, calls=%fused_computation.66 | convolution fusion | flops 5043388416 | bytes 26765312 | tf_op jit(solution)/shard_map/dot_general | solution.py:17
  350.4 15.8 %all-gather.17.cloned.1.call-done = bf16[3072,768]{1,0:T(8,128)(2,1)} async-done(((bf16[96,768]{1,0:T(8,128)(2,1)}), bf16[3072,768]{1,0:T(8,128)(2,1)}) %all-gather.17.cloned.1.call-update) | async-done | bytes 4718608 | tf_op jit(solution)/shard_map/all_gather | solution.py:123
  366.2 8.9 fusion.85
  382.3 13.5 %convert_reduce_fusion = (f32[3072]{0:T(1024)}, bf16[1024,3072]{1,0:T(8,128)(2,1)S(1)}) fusion(f32[1024,3072]{1,0:T(8,128)} %get-tuple-element.287, f32[3072]{0:T(1024)S(1)} %convert_element_type.117, bf16[3072,768]{1,0:T(8,128)(2,1)S(1)} %bitcast.189, f32[1024,768]{0,1:T(8,128)S(1)} %get-tuple-element.276), kind=kOutput, calls=%fused_computation.73 | convolution fusion | flops 4873516032 | bytes 26763264 | tf_op jit(solution)/shard_map/dot_general | solution.py:27
  395.8 6.6 multiply_reduce_fusion.2
  419.5 52.0 %while.27 = (s32[]{:T(128)}, bf16[2,512,12,64]{1,3,2,0:T(8,128)(2,1)}, bf16[2,512,12,64]{1,3,2,0:T(8,128)(2,1)}, bf16[2,512,12,64]{1,3,2,0:T(8,128)(2,1)}, bf16[...) while((s32[]{:T(128)}, ...), condition=%wide.region_14.15_spmd, body=%wide.region_12.14_spmd.sunk | while | flops 2062412288 | bytes 140180784 | solution.py:330
  422.9 7.3 multiply_reduce_fusion.10
  430.2 7.4 multiply_convert_fusion.4
  441.9 3.8 fusion.151
  448.8 7.3 multiply_reduce_fusion.10
  456.2 7.2 multiply_convert_fusion.4
  467.8 3.8 fusion.151
  501.3 10.6 fusion.80
  512.2 10.4 fusion.77
  525.7 40.5 %all-reduce.18 = (f32[768]{0:T(1024)S(1)}, f32[768]{0:T(1024)S(1)}, f32[768]{0:T(1024)S(1)}, f32[768]{0:T(1024)S(1)}, f32[768]{0:T(1024)S(1)}, /*index=5*/f32[30...) all-reduce(f32[768]{0:T(1024)S(1)} %reduce_sum.184, ...), channel_id=6, replica_groups=mesh['dp'=4,'fsdp'=8] {'dp','fsdp'}, use_global_device_ids=true, to_apply=%region_20.21.clone | all-reduce | flops 9216 | bytes 73728
  580.1 3.7 copy.119
  586.7 31.5 %reduce-scatter.19.cloned.1.call-done = f32[24,768]{1,0:T(8,128)} async-done(((f32[768,768]{1,0:T(8,128)}), f32[24,768]{1,0:T(8,128)}) %reduce-scatter.19.cloned.1.call-update) | async-done | bytes 73744
  618.2 103.9 %reduce-scatter.21.cloned.1.call-done = f32[24,768]{1,0:T(8,128)} async-done(((f32[768,768]{1,0:T(8,128)}), f32[24,768]{1,0:T(8,128)}) %reduce-scatter.21.cloned.1.call-update) | async-done | bytes 73744
  722.1 104.6 %reduce-scatter.23.cloned.1.call-done = f32[24,768]{1,0:T(8,128)} async-done(((f32[768,768]{1,0:T(8,128)}), f32[24,768]{1,0:T(8,128)}) %reduce-scatter.23.cloned.1.call-update) | async-done | bytes 73744
  826.8 141.1 %reduce-scatter.15.cloned.1.call-done = f32[24,3072]{1,0:T(8,128)} async-done(((f32[768,3072]{1,0:T(8,128)}), f32[24,3072]{1,0:T(8,128)}) %reduce-scatter.15.cloned.1.call-update) | async-done | bytes 294928 | tf_op jit(solution)/shard_map/reduce_scatter | solution.py:195
  967.9 141.9 %reduce-scatter.17.cloned.1.call-done = f32[96,768]{1,0:T(8,128)} async-done(((f32[3072,768]{1,0:T(8,128)}), f32[96,768]{1,0:T(8,128)}) %reduce-scatter.17.cloned.1.call-update) | async-done | bytes 294928 | tf_op jit(solution)/shard_map/reduce_scatter | solution.py:197
  (296 shorter events, 140.8 us)
Async XLA Ops:
  7.2 7.3 copy-start.12
  7.2 60.7 %all-gather.7.cloned.1.call-start = ((), (), s32[]{:S(2)}) async-start(), calls=%async_computation.6 | async-start | bytes 1216512 | tf_op jit(solution)/shard_map/all_gather | solution.py:114
  7.9 116.1 %all-gather.9.cloned.1.call-start = ((), (), s32[]{:S(2)}) async-start(), calls=%async_computation.7 | async-start | bytes 1216512 | tf_op jit(solution)/shard_map/all_gather | solution.py:112
  8.7 171.2 %all-gather.11.cloned.1.call-start = ((), (), s32[]{:S(2)}) async-start(), calls=%async_computation.8 | async-start | bytes 1216512 | tf_op jit(solution)/shard_map/all_gather | solution.py:113
  9.4 226.2 %all-gather.13.cloned.1.call-start = ((), (), s32[]{:S(2)}) async-start(), calls=%async_computation.9 | async-start | bytes 1216512 | tf_op jit(solution)/shard_map/all_gather | solution.py:115
  10.0 291.0 %all-gather.15.cloned.1.call-start = ((), (), s32[]{:S(2)}) async-start(), calls=%async_computation.10 | async-start | bytes 4866048 | tf_op jit(solution)/shard_map/all_gather | solution.py:121
  10.6 355.6 %all-gather.17.cloned.1.call-start = ((), (), s32[]{:S(2)}) async-start(), calls=%async_computation.11 | async-start | bytes 4866048 | tf_op jit(solution)/shard_map/all_gather | solution.py:123
  11.2 575.6 %reduce-scatter.13.cloned.1.call-start = ((), (), s32[]{:S(2)}) async-start(), calls=%async_computation.12 | async-start | bytes 2433024 | tf_op jit(solution)/shard_map/reduce_scatter | solution.py:189
  61.4 340.9 %copy-start.39 = (f32[768]{0:T(1024)}, f32[768]{0:T(1024)S(1)}, u32[]{:S(2)}) copy-start(f32[768]{0:T(1024)S(1)} %convert_element_type.114) | copy-start | bytes 9220
  61.4 304.8 %copy-start.46 = (f32[768]{0:T(1024)}, f32[768]{0:T(1024)S(1)}, u32[]{:S(2)}) copy-start(f32[768]{0:T(1024)S(1)} %convert_element_type.115) | copy-start | bytes 9220
  62.6 5.3 copy-start.27
  72.5 51.4 %copy-start.28 = (bf16[1024,768]{1,0:T(8,128)(2,1)S(1)}, bf16[1024,768]{1,0:T(8,128)(2,1)}, u32[]{:S(2)}) copy-start(bf16[1024,768]{1,0:T(8,128)(2,1)} %convert_element_type.107) | copy-start | bytes 4718596
  214.0 5.7 copy-start
  214.0 5.7 copy-start.2
  214.0 5.7 copy-start.32
  239.9 162.4 %copy-start.14 = (f32[1024,768]{0,1:T(8,128)}, f32[1024,768]{0,1:T(8,128)S(1)}, u32[]{:S(2)}) copy-start(f32[1024,768]{0,1:T(8,128)S(1)} %get-tuple-element.285) | copy-start | bytes 9437188
  239.9 162.4 %copy-start.35 = (f32[1024]{0:T(1024)}, f32[1024]{0:T(1024)S(1)}, u32[]{:S(2)}) copy-start(f32[1024]{0:T(1024)S(1)} %broadcast_multiply_fusion.5) | copy-start | bytes 12292
  240.3 162.0 %copy-start.41 = (f32[1024]{0:T(1024)}, f32[1024]{0:T(1024)S(1)}, u32[]{:S(2)}) copy-start(f32[1024]{0:T(1024)S(1)} %add_rsqrt_fusion.1) | copy-start | bytes 12292
  240.3 125.9 %copy-start.48 = (f32[768]{0:T(1024)S(1)}, f32[768]{0:T(1024)}, u32[]{:S(2)}) copy-start(f32[768]{0:T(1024)} %convert_element_type.119) | copy-start | bytes 9220
  377.0 5.2 slice-start.2
  378.8 17.0 %slice-start = ((s8[4718592]{0:T(1024)(128)(4,1)}), s8[524288]{0:T(1024)(128)(4,1)S(1)}, s32[]{:S(2)}) async-start(s8[4718592]{0:T(1024)(128)(4,1)} %bitcast.186), calls=%async_computation.18 | async-start | bytes 1048576
  382.2 13.5 %copy-start.22 = (f32[1024,768]{0,1:T(8,128)}, f32[1024,768]{0,1:T(8,128)S(1)}, u32[]{:S(2)}) copy-start(f32[1024,768]{0,1:T(8,128)S(1)} %get-tuple-element.276) | copy-start | bytes 9437188
  382.2 13.5 %slice-start.1 = ((s8[4718592]{0:T(1024)(128)(4,1)}), s8[4194304]{0:T(1024)(128)(4,1)S(1)}, s32[]{:S(2)}) async-start(s8[4718592]{0:T(1024)(128)(4,1)} %bitcast.186), calls=%async_computation.19 | async-start | bytes 8388608
  395.7 6.6 copy-start.64
  415.5 202.7 %reduce-scatter.19.cloned.1.call-start = ((), (), s32[]{:S(2)}) async-start(), calls=%async_computation.15 | async-start | bytes 2433024
  430.2 7.4 copy-start.19
  456.2 7.2 copy-start.19
  471.6 4.7 copy-start.29
  482.4 239.7 %reduce-scatter.21.cloned.1.call-start = ((), (), s32[]{:S(2)}) async-start(), calls=%async_computation.16 | async-start | bytes 2433024
  492.0 334.8 %reduce-scatter.23.cloned.1.call-start = ((), (), s32[]{:S(2)}) async-start(), calls=%async_computation.17 | async-start | bytes 2433024
  501.2 466.7 %reduce-scatter.15.cloned.1.call-start = ((), (), s32[]{:S(2)}) async-start(), calls=%async_computation.13 | async-start | bytes 9732096 | tf_op jit(solution)/shard_map/reduce_scatter | solution.py:195
  511.9 597.9 %reduce-scatter.17.cloned.1.call-start = ((), (), s32[]{:S(2)}) async-start(), calls=%async_computation.14 | async-start | bytes 9732096 | tf_op jit(solution)/shard_map/reduce_scatter | solution.py:197
  (56 other events, 157.2 us)
Sparse Core Ops, SparseCore 0:
  10.9 56.9 all-gather.6
  70.8 53.1 all-gather.8
  126.9 52.9 all-gather.10
  182.6 52.9 all-gather.12
  238.4 62.5 all-gather.14
  303.8 62.4 all-gather.16
  415.6 97.7 reduce-scatter.12
  520.1 98.0 reduce-scatter.18
  624.1 97.9 reduce-scatter.20
  728.7 98.0 reduce-scatter.22
  833.2 134.6 reduce-scatter.14
  975.2 134.5 reduce-scatter.16
where the time goes:
time: 1130 us; the launch traced here: 1120 us
  waiting for transfers between devices  721 us (64%)
  matrix products  182 us (16%)
  blocking collectives  82.9 us (7%)
  local copies, waits for them, and re-layouts  75.7 us (7%)
  other arithmetic  37.9 us (3%)
  between operations  15.4 us (1%)
    unnamed x15, waiting for transfers between devices  244 us
    reduce_scatter x1, waiting for transfers between devices, settle_grads(): lax.psum_scatter(down_weight, ('dp', 'fsdp'), scatter_dimension=0, tiled=...  142 us
    reduce_scatter x1, waiting for transfers between devices, settle_grads(): lax.psum_scatter(inner_weight, ('dp', 'fsdp'), scatter_dimension=0, tiled...  141 us
    unnamed x2, blocking collectives  82.9 us
    dot_general x6, matrix products, product(): return jnp.dot(lhs_rows, rhs_cols, preferred_element_type=jnp.float32)  72.1 us
    all_gather x1, waiting for transfers between devices, gather_first(): lax.all_gather(inner_weight, ('dp', 'fsdp'), axis=0, tiled=True)  60.7 us
    all_gather x1, waiting for transfers between devices, gather_first(): lax.all_gather(key_weight, ('dp', 'fsdp'), axis=0, tiled=True)  50.9 us
    all_gather x1, waiting for transfers between devices, gather_first(): lax.all_gather(query_weight, ('dp', 'fsdp'), axis=0, tiled=True)  49.9 us
  transfers between devices with their start and end apart: 12, of which 11 were waited for; matrix products, arithmetic and copies ran while one was open for 21% of the time, Pallas kernels for 0%

commit v1 on v0

v1 whole, which is shorter than its diff:
```python
import functools
import math

import jax
import jax.numpy as jnp
from jax import lax
from jax.experimental import pallas as pl
from jax.experimental.pallas import tpu as pltpu
from jax.sharding import PartitionSpec as P

D = 768
H = 12
DH = 64
FF = 3072
SLABS = 32
SLAB = D // SLABS
CHIPS = SLABS // 2
PAIR_ROWS = 2 * SLAB
NORM_EPSILON = 1e-12
MASKED_SCORE = -1000000000.0
GAUSS_DENSITY = 0.3989422804014327
LOG2E = 1.4426950408889634
MIB = 1 << 20

QKV_HALF = 3 * D // 2
QKV_BLOCK = QKV_HALF + 128
OUT_HALF = D // 2
INNER_HALF = FF // 2
FFN_BLOCK = OUT_HALF + INNER_HALF + 2 * D

bf16 = jnp.bfloat16
f32 = jnp.float32
ANY = pl.BlockSpec(memory_space=pl.ANY)
SMEM = pl.BlockSpec(memory_space=pltpu.SMEM)


def dot(a, b):
    return lax.dot_general(a, b, (((1,), (0,)), ((), ())), preferred_element_type=f32)


def dot_t(a, b):
    return lax.dot_general(a, b, (((1,), (1,)), ((), ())), preferred_element_type=f32)


def dot_l(a, b):
    return lax.dot_general(a, b, (((0,), (0,)), ((), ())), preferred_element_type=f32)


def aligned(start, size, unit):
    return pl.ds(pl.multiple_of(start, unit), size)


def qkv_blocks(place, pieces, weights, sem):
    chip, core = place[0], place[1]
    for ref, chips, other in pieces:
        half = 1 - core if other else core
        for slot, rel in enumerate(chips):
            rows = aligned((chip ^ rel) * PAIR_ROWS, PAIR_ROWS, 16)
            yield pltpu.make_async_copy(
                ref.at[slot], weights.at[rows, aligned(half * QKV_BLOCK, QKV_BLOCK, 128)], sem
            )


def ffn_blocks(place, pieces, out_w, inner_w, down_w, sem):
    chip, core = place[0], place[1]
    for ref, chips, other in pieces:
        half = 1 - core if other else core
        for slot, rel in enumerate(chips):
            owner = chip ^ rel
            rows = aligned(owner * PAIR_ROWS, PAIR_ROWS, 16)
            start = OUT_HALF + INNER_HALF
            yield pltpu.make_async_copy(
                ref.at[slot, :, pl.ds(0, OUT_HALF)],
                out_w.at[rows, aligned(half * OUT_HALF, OUT_HALF, 128)],
                sem,
            )
            yield pltpu.make_async_copy(
                ref.at[slot, :, pl.ds(OUT_HALF, INNER_HALF)],
                inner_w.at[rows, aligned(half * INNER_HALF, INNER_HALF, 128)],
                sem,
            )
            for i in range(2):
                down_rows = (owner * 2 + half) * (2 * PAIR_ROWS) + i * PAIR_ROWS
                yield pltpu.make_async_copy(
                    ref.at[slot, :, pl.ds(start + i * D, D)],
                    down_w.at[aligned(down_rows, PAIR_ROWS, 16), :],
                    sem,
                )


class ToCore:
    def __init__(self, source, keep, send, sem, other):
        self.source, self.keep, self.send, self.sem, self.other = source, keep, send, sem, other

    def start(self):
        @pl.when(self.other == 0)
        def _():
            pltpu.make_async_copy(self.source, self.keep, self.sem).start()

        @pl.when(self.other == 1)
        def _():
            pltpu.make_async_copy(self.source, self.send, self.sem).start()

    def wait(self):
        pltpu.make_async_copy(self.source, self.keep, self.sem).wait()


def lane_masks():
    low = (lax.broadcasted_iota(jnp.int32, (1, 128), 1) < DH).astype(f32)
    return low.astype(bf16), (1.0 - low).astype(bf16)


def attend_kernel(meta, n_pieces, place, lengths, x_ref, *refs):
    piece_refs = refs[:n_pieces]
    qkv_ref, att_ref, stat_ref, weights, vectors = refs[n_pieces : n_pieces + 5]
    sem = refs[-1]
    seq = pl.program_id(0)
    rows = x_ref.shape[0]

    @pl.when(seq == 0)
    def _():
        copies = list(qkv_blocks(place, [(r,) + m for r, m in zip(piece_refs, meta)], weights, sem))
        for c in copies:
            c.start()
        for c in copies:
            c.wait()
        small = weights[:, QKV_HALF:QKV_BLOCK].astype(f32)
        vectors[...] = small.T[0:16, :]

    lowered = x_ref[...].astype(bf16)
    first = dot(lowered, weights[:, 0:QKV_HALF])
    qkv_ref[:, 0:D] = (first[:, 0:D] + vectors[0:1, :]).astype(bf16)
    qkv_ref[:, D:QKV_HALF] = first[:, D:QKV_HALF].astype(bf16)
    second = dot(lowered, weights[:, QKV_BLOCK : QKV_BLOCK + QKV_HALF])
    qkv_ref[:, QKV_HALF : 2 * D] = second[:, 0 : D // 2].astype(bf16)
    qkv_ref[:, 2 * D :] = (second[:, D // 2 :] + vectors[1:2, :]).astype(bf16)

    low, high = lane_masks()
    lane = lax.broadcasted_iota(jnp.int32, (1, 128), 1)
    key_at = lax.broadcasted_iota(jnp.int32, (1, rows), 1)
    hidden_keys = jnp.where(key_at < lengths[seq], 0.0, MASKED_SCORE).astype(f32)
    chunk = 256
    ones = jnp.ones((rows, 128), bf16)
    stats = [jnp.zeros((chunk, 128), f32) for _ in range(rows // chunk)]
    for pair in range(H // 2):
        at = pair * 128
        keys = qkv_ref[:, D + at : D + at + 128]
        values = jnp.concatenate([qkv_ref[:, 2 * D + at : 2 * D + at + 128], ones], axis=1)
        keys_of = (keys * low, keys * high)
        for c in range(rows // chunk):
            span = pl.ds(c * chunk, chunk)
            queries = qkv_ref[span, at : at + 128]
            outs = []
            for i in range(2):
                scores = dot_t(queries, keys_of[i]) * (0.125 * LOG2E) + hidden_keys
                peak = jnp.max(scores, axis=-1, keepdims=True)
                weight = jnp.exp2(scores - peak).astype(bf16)
                both = dot(weight, values)
                total = both[:, 128:]
                outs.append(both[:, :128] / total)
                log_total = peak + jnp.log2(total)
                stats[c] = jnp.where(lane == 2 * pair + i, log_total, stats[c])
            att_ref[span, at : at + 128] = jnp.where(lane < DH, outs[0], outs[1]).astype(bf16)
    for c in range(rows // chunk):
        stat_ref[0, :, c * chunk : (c + 1) * chunk] = stats[c].T[0:16, :]


def attend(place, lengths, x, pieces, meta):
    rows = x.shape[0] // lengths.shape[0]
    seqs = lengths.shape[0]
    whole = lambda *shape: pl.BlockSpec(shape, lambda s: (0,) * len(shape))
    return pl.pallas_call(
        functools.partial(attend_kernel, meta, len(pieces)),
        grid=(seqs,),
        in_specs=[SMEM, SMEM, pl.BlockSpec((rows, D), lambda s: (s, 0))] + [ANY] * len(pieces),
        out_specs=[
            pl.BlockSpec((rows, 3 * D), lambda s: (s, 0)),
            pl.BlockSpec((rows, D), lambda s: (s, 0)),
            pl.BlockSpec((1, 16, rows), lambda s: (s, 0, 0)),
            whole(D, 2 * QKV_BLOCK),
            whole(16, D),
        ],
        out_shape=[
            jax.ShapeDtypeStruct((seqs * rows, 3 * D), bf16),
            jax.ShapeDtypeStruct((seqs * rows, D), bf16),
            jax.ShapeDtypeStruct((seqs, 16, rows), f32),
            jax.ShapeDtypeStruct((D, 2 * QKV_BLOCK), bf16),
            jax.ShapeDtypeStruct((16, D), f32),
        ],
        scratch_shapes=[pltpu.SemaphoreType.DMA],
        compiler_params=pltpu.CompilerParams(vmem_limit_bytes=56 * MIB),
        cost_estimate=pl.CostEstimate(
            flops=2 * seqs * rows * D * 3 * D, bytes_accessed=20 * MIB, transcendentals=H * seqs * rows * rows
        ),
        name="attend",
    )(place, lengths, x, *pieces)


def gelu_parts(u):
    size = jnp.abs(u)
    bell = jnp.exp2(u * u * (-0.5 * LOG2E))
    t = 1.0 / (1.0 + (0.3275911 * math.sqrt(0.5)) * size)
    poly = t * (0.127414796 + t * (-0.142248368 + t * (0.7107068705 + t * (-0.7265760135 + t * 0.5307027145))))
    tail = poly * bell
    below = jnp.where(u < 0.0, tail, 1.0 - tail)
    return below, bell


def mean_rows(v):
    return jnp.sum(v, axis=-1, keepdims=True) * (1.0 / D)


def norm_rows(total):
    center = total - mean_rows(total)
    rstd = lax.rsqrt(mean_rows(center * center) + NORM_EPSILON)
    return center * rstd, rstd


def norm_back(upstream, normed, rstd, gain):
    scaled = upstream * gain
    return rstd * (scaled - mean_rows(scaled) - normed * mean_rows(scaled * normed))


BLOCK = 256
PAYLOAD_ROWS = 224
DOWN_STEPS = 8
INNER_STEPS = 2


def ffn_kernel(meta, n_pieces, blocks, place, x_ref, att_ref, cot_ref, vec_ref, b1_ref, *refs):
    piece_refs = refs[:n_pieces]
    (out_ref, fb_ref, ab_ref, small_ref, db1_ref, keep, send) = refs[n_pieces : n_pieces + 7]
    (out_w, inner_w, down_w, act, inner_back, hid, down_back, att, branch, slope, grad, stage, sem, wsem) = refs[
        n_pieces + 7 :
    ]
    step = pl.program_id(0)
    me = place[0] * 2 + place[1]
    down_at, inner_at, out_at = blocks, blocks + DOWN_STEPS, blocks + DOWN_STEPS + INNER_STEPS

    @pl.when(step == 0)
    def _():
        copies = list(ffn_blocks(place, [(r,) + m for r, m in zip(piece_refs, meta)], out_w, inner_w, down_w, sem))
        for c in copies:
            c.start()
        for c in copies:
            c.wait()
        small_ref[...] = jnp.zeros_like(small_ref)
        db1_ref[...] = jnp.zeros_like(db1_ref)

    @pl.when(step < blocks)
    def _():
        rows = aligned(step * BLOCK, BLOCK, BLOCK)
        attended = att_ref[...]
        att[rows, :] = attended
        first_gain, first_shift = vec_ref[3:4, :], vec_ref[4:5, :]
        second_gain, second_shift = vec_ref[6:7, :], vec_ref[7:8, :]
        first_normed, first_rstd = norm_rows(x_ref[...] + dot(attended, out_w[...]) + vec_ref[2:3, :])
        hidden = first_normed * first_gain + first_shift
        hidden_low = hidden.astype(bf16)
        hid[rows, :] = hidden_low
        total = hidden + vec_ref[5:6, :]
        for c in range(FF // D):
            cols = pl.ds(c * D, D)
            u = dot(hidden_low, inner_w[:, cols]) + b1_ref[:, cols]
            below, bell = gelu_parts(u)
            active = (u * below).astype(bf16)
            act[rows, cols] = active
            slope[:, cols] = below + u * bell * GAUSS_DENSITY
            total = total + dot(active, down_w[cols, :])
        second_normed, second_rstd = norm_rows(total)
        out_ref[...] = second_normed * second_gain + second_shift
        cot = cot_ref[...]
        second_back = norm_back(cot, second_normed, second_rstd, second_gain)
        back_low = second_back.astype(bf16)
        down_back[rows, :] = back_low
        hidden_back = second_back
        for c in range(FF // D):
            cols = pl.ds(c * D, D)
            ib = (dot_t(back_low, down_w[cols, :]) * slope[:, cols]).astype(bf16)
            inner_back[rows, cols] = ib
            db1_ref[:, cols] += jnp.sum(ib.astype(f32), axis=0, keepdims=True)
            hidden_back = hidden_back + dot_t(ib, inner_w[:, cols])
        first_back = norm_back(hidden_back, first_normed, first_rstd, first_gain)
        fb_ref[...] = first_back
        branch_low = first_back.astype(bf16)
        branch[rows, :] = branch_low
        ab_ref[...] = dot_t(branch_low, out_w[...]).astype(bf16)
        sums = (
            branch_low.astype(f32),
            hidden_back * first_normed,
            hidden_back,
            back_low.astype(f32),
            cot * second_normed,
            cot,
        )
        for i, v in enumerate(sums):
            small_ref[2 + i : 3 + i, :] += jnp.sum(v, axis=0, keepdims=True)

    def store(slab, first_row, count, slot):
        source = stage.at[slot, pl.ds(0, count)]
        place_in = lambda ref: ref.at[(slab ^ me) >> 1, pl.ds(first_row, count)]
        return ToCore(source, place_in(keep), place_in(send), wsem.at[slot], (slab ^ me) & 1)

    @pl.when((step >= down_at) & (step < inner_at))
    def _():
        chunk = step - down_at
        width = FF // DOWN_STEPS
        per = SLABS // DOWN_STEPS
        g = dot_l(act[:, aligned(chunk * width, width, 128)], down_back[...])
        for i in range(per):
            slab = chunk * per + i

            @pl.when(chunk > 0)
            def _():
                store(slab, 0, 4 * SLAB, i).wait()

            stage[i, 0 : 4 * SLAB, :] = g[i * 4 * SLAB : (i + 1) * 4 * SLAB, :].astype(bf16)
            store(slab, 0, 4 * SLAB, i).start()

        @pl.when(chunk == DOWN_STEPS - 1)
        def _():
            for i in range(per):
                store(0, 0, 4 * SLAB, i).wait()

    def pack(first_row, count):
        def body(k, _):
            for i in range(4):
                slab = k * 4 + i

                @pl.when(k > 0)
                def _():
                    store(slab, first_row, count, i).wait()

                rows = aligned(slab * SLAB, SLAB, 8)
                parts = [grad[j, rows, :] for j in range(2)]
                stage[i, 0:count, :] = jnp.concatenate(parts, axis=0)[0:count].astype(bf16)
                store(slab, first_row, count, i).start()
            return 0

        lax.fori_loop(0, SLABS // 4, body, 0)
        for i in range(4):
            store(0, first_row, count, i).wait()

    @pl.when((step >= inner_at) & (step < out_at))
    def _():
        half = step - inner_at
        for j in range(2):
            grad[j] = dot_l(hid[...], inner_back[:, aligned(half * 2 * D + j * D, D, 128)])
        pack(4 * SLAB + half * 2 * SLAB, 2 * SLAB)

    @pl.when(step == out_at)
    def _():
        grad[0] = dot_l(att[...], branch[...])
        grad[1] = jnp.zeros((D, D), f32)
        pack(8 * SLAB, 32)


def feed_forward(place, x, attended, cotangent, vectors, inner_bias, pieces, meta):
    count = x.shape[0]
    blocks = count // BLOCK
    last = blocks - 1
    token = lambda: pl.BlockSpec((BLOCK, D), lambda s: (jnp.minimum(s, last), 0))
    whole = lambda *shape: pl.BlockSpec(shape, lambda s: (0,) * len(shape))
    return pl.pallas_call(
        functools.partial(ffn_kernel, meta, len(pieces), blocks),
        grid=(blocks + DOWN_STEPS + INNER_STEPS + 1,),
        in_specs=[SMEM, token(), token(), token(), whole(16, D), whole(1, FF)] + [ANY] * len(pieces),
        out_specs=[token(), token(), token(), whole(8, D), whole(1, FF), ANY, ANY],
        out_shape=[
            jax.ShapeDtypeStruct((count, D), f32),
            jax.ShapeDtypeStruct((count, D), f32),
            jax.ShapeDtypeStruct((count, D), bf16),
            jax.ShapeDtypeStruct((8, D), f32),
            jax.ShapeDtypeStruct((1, FF), f32),
            jax.ShapeDtypeStruct((CHIPS, PAYLOAD_ROWS, D), bf16),
            jax.ShapeDtypeStruct((CHIPS, PAYLOAD_ROWS, D), bf16),
        ],
        scratch_shapes=[
            pltpu.VMEM((D, D), bf16),
            pltpu.VMEM((D, FF), bf16),
            pltpu.VMEM((FF, D), bf16),
            pltpu.VMEM((count, FF), bf16),
            pltpu.VMEM((count, FF), bf16),
            pltpu.VMEM((count, D), bf16),
            pltpu.VMEM((count, D), bf16),
            pltpu.VMEM((count, D), bf16),
            pltpu.VMEM((count, D), bf16),
            pltpu.VMEM((BLOCK, FF), f32),
            pltpu.VMEM((2, D, D), f32),
            pltpu.VMEM((4, 4 * SLAB, D), bf16),
            pltpu.SemaphoreType.DMA,
            pltpu.SemaphoreType.DMA((4,)),
        ],
        compiler_params=pltpu.CompilerParams(vmem_limit_bytes=62 * MIB),
        cost_estimate=pl.CostEstimate(
            flops=12 * count * D * FF + 6 * count * D * D, bytes_accessed=40 * MIB, transcendentals=2 * count * FF
        ),
        name="feed_forward",
    )(place, x, attended, cotangent, vectors, inner_bias, *pieces)


def attend_back_kernel(seqs, place, lengths, x_ref, qkv_ref, back_ref, stat_ref, small_ref, db1_ref, *refs):
    (grads_out, keep, send, grads, lowered, grad, stage, sem, wsem) = refs
    step = pl.program_id(0)
    pairs = H // 2
    rows = x_ref.shape[0]
    me = place[0] * 2 + place[1]
    low, high = lane_masks()
    chunk = 256

    @pl.when(step < seqs * pairs)
    def _():
        seq, pair = step // pairs, step % pairs
        at = pair * 128

        @pl.when(pair == 0)
        def _():
            lowered[aligned(seq * rows, rows, rows), :] = x_ref[...].astype(bf16)

        queries = qkv_ref[:, aligned(at, 128, 128)]
        keys = qkv_ref[:, aligned(D + at, 128, 128)]
        values = qkv_ref[:, aligned(2 * D + at, 128, 128)]
        upstream = back_ref[:, aligned(at, 128, 128)]
        key_at = lax.broadcasted_iota(jnp.int32, (rows, 1), 0)
        hidden_keys = jnp.where(key_at < lengths[seq], 0.0, MASKED_SCORE).astype(f32)
        query_back = [jnp.zeros((chunk, 128), f32) for _ in range(rows // chunk)]
        key_back = jnp.zeros((rows, 128), f32)
        value_back = jnp.zeros((rows, 128), f32)
        for i, mask in enumerate((low, high)):
            own_keys, own_values = keys * mask, values * mask
            own_queries, own_up = queries * mask, upstream * mask
            for c in range(rows // chunk):
                span = slice(c * chunk, (c + 1) * chunk)
                log_total = stat_ref[0, pl.ds(2 * pair + i, 1), span]
                scores = dot_t(own_keys, queries[span]) * (0.125 * LOG2E) + hidden_keys
                weight = jnp.exp2(scores - log_total)
                weight_back = dot_t(own_values, upstream[span])
                mean = jnp.sum(weight * weight_back, axis=0, keepdims=True)
                score_back = (weight * (weight_back - mean)).astype(bf16)
                value_back += dot(weight.astype(bf16), own_up[span])
                key_back += dot(score_back, own_queries[span])
                query_back[c] += dot_l(score_back, own_keys)
        to = seq * rows
        for c in range(rows // chunk):
            grads[aligned(to + c * chunk, chunk, chunk), aligned(at, 128, 128)] = (query_back[c] * 0.125).astype(bf16)
        grads[aligned(to, rows, rows), aligned(D + at, 128, 128)] = (key_back * 0.125).astype(bf16)
        grads[aligned(to, rows, rows), aligned(2 * D + at, 128, 128)] = value_back.astype(bf16)

    whole_copy = pltpu.make_async_copy(grads, grads_out, sem)

    @pl.when(step == seqs * pairs)
    def _():
        whole_copy.start()

    @pl.when(step >= seqs * pairs)
    def _():
        which = step - seqs * pairs
        grad[which] = dot_l(lowered[...], grads[:, aligned(which * D, D, 128)])

    def store(slab, slot):
        rel = slab ^ me
        return ToCore(stage.at[slot], keep.at[rel >> 1], send.at[rel >> 1], wsem.at[slot], rel & 1)

    @pl.when(step == seqs * pairs + 2)
    def _():
        query_bias = jnp.sum(grads[:, 0:D].astype(f32), axis=0, keepdims=True)
        value_bias = jnp.sum(grads[:, 2 * D :].astype(f32), axis=0, keepdims=True)
        rows_of = jnp.concatenate([query_bias, value_bias, small_ref[2:8, :], jnp.zeros((120, D), f32)], axis=0)
        columns = rows_of.T
        owner = lax.broadcasted_iota(jnp.int32, (SLABS, FF), 1) // (4 * SLAB)
        mine = jnp.where(owner == lax.broadcasted_iota(jnp.int32, (SLABS, FF), 0), db1_ref[...], 0.0)
        place_of = lax.broadcasted_iota(jnp.int32, (FF, 128), 0) % (4 * SLAB)
        pick = (place_of == lax.broadcasted_iota(jnp.int32, (FF, 128), 1)).astype(f32)
        table = lax.dot_general(
            mine, pick, (((1,), (0,)), ((), ())), precision=lax.Precision.HIGHEST, preferred_element_type=f32
        )
        for slab in range(SLABS):
            slot = slab % 4
            if slab >= 4:
                store(slab, slot).wait()
            at = slab * SLAB
            lanes = [columns[at + 8 * i : at + 8 * i + 8, :] for i in range(3)]
            lanes.append(jnp.broadcast_to(table[slab : slab + 1, :], (8, 128)))
            lanes.append(jnp.zeros((8, 256), f32))
            parts = [grad[j, at : at + SLAB, :] for j in range(3)] + [jnp.concatenate(lanes, axis=1)]
            stage[slot] = jnp.concatenate(parts, axis=0).astype(bf16)
            store(slab, slot).start()
        for slot in range(4):
            store(0, slot).wait()
        whole_copy.wait()


def attend_back(place, lengths, x, qkv, back, stats, small, inner_bias_grad):
    seqs = lengths.shape[0]
    rows = x.shape[0] // seqs
    pairs = H // 2
    seq_of = lambda s: jnp.minimum(s // pairs, seqs - 1)
    whole = lambda *shape: pl.BlockSpec(shape, lambda s: (0,) * len(shape))
    return pl.pallas_call(
        functools.partial(attend_back_kernel, seqs),
        grid=(seqs * pairs + 3,),
        in_specs=[
            SMEM,
            SMEM,
            pl.BlockSpec((rows, D), lambda s: (seq_of(s), 0)),
            pl.BlockSpec((rows, 3 * D), lambda s: (seq_of(s), 0)),
            pl.BlockSpec((rows, D), lambda s: (seq_of(s), 0)),
            pl.BlockSpec((1, 16, rows), lambda s: (seq_of(s), 0, 0)),
            whole(8, D),
            whole(1, FF),
        ],
        out_specs=[ANY, ANY, ANY],
        out_shape=[
            jax.ShapeDtypeStruct((seqs * rows, 3 * D), bf16),
            jax.ShapeDtypeStruct((CHIPS, 80, D), bf16),
            jax.ShapeDtypeStruct((CHIPS, 80, D), bf16),
        ],
        scratch_shapes=[
            pltpu.VMEM((seqs * rows, 3 * D), bf16),
            pltpu.VMEM((seqs * rows, D), bf16),
            pltpu.VMEM((3, D, D), f32),
            pltpu.VMEM((4, 80, D), bf16),
            pltpu.SemaphoreType.DMA,
            pltpu.SemaphoreType.DMA((4,)),
        ],
        compiler_params=pltpu.CompilerParams(vmem_limit_bytes=56 * MIB),
        cost_estimate=pl.CostEstimate(
            flops=2 * seqs * rows * D * 3 * D, bytes_accessed=30 * MIB, transcendentals=H * seqs * rows * rows
        ),
        name="attend_back",
    )(place, lengths, x, qkv, back, stats, small, inner_bias_grad)


def input_back_kernel(fb_ref, grads_ref, w_ref, out_ref):
    half = D + D // 2
    first = dot_t(grads_ref[:, 0:half], w_ref[:, 0:half])
    second = dot_t(grads_ref[:, half:], w_ref[:, QKV_BLOCK : QKV_BLOCK + half])
    out_ref[...] = fb_ref[...] + first + second


def input_back(first_back, grads, weights):
    count = first_back.shape[0]
    return pl.pallas_call(
        input_back_kernel,
        grid=(count // BLOCK,),
        in_specs=[
            pl.BlockSpec((BLOCK, D), lambda s: (s, 0)),
            pl.BlockSpec((BLOCK, 3 * D), lambda s: (s, 0)),
            pl.BlockSpec((D, 2 * QKV_BLOCK), lambda s: (0, 0)),
        ],
        out_specs=pl.BlockSpec((BLOCK, D), lambda s: (s, 0)),
        out_shape=jax.ShapeDtypeStruct((count, D), f32),
        compiler_params=pltpu.CompilerParams(vmem_limit_bytes=56 * MIB),
        cost_estimate=pl.CostEstimate(flops=6 * count * D * D, bytes_accessed=15 * MIB, transcendentals=0),
        name="input_back",
    )(first_back, grads, weights)


AXES = ("dp", "fsdp")


def swap(v, mask, count):
    return lax.ppermute(v, AXES, [(i, i ^ mask) for i in range(count)])


CORE, ALONG_X, ALONG_Y, ALONG_Z = 1, 2, 4, 8
Z_COUNT = 4
FAST_SHAPE = {"dp": Z_COUNT, "fsdp": 8}


def gather_group(block):
    move = lambda v, mask: swap(v, mask, SLABS)
    per_z = [block] + [move(block, k * ALONG_Z) for k in range(1, Z_COUNT)]
    first, second = jnp.stack(per_z[:2]), jnp.stack(per_z[2:])
    first_chips, second_chips = (0, 4), (8, 12)
    shift = lambda chips, by: tuple(c ^ by for c in chips)
    first = jnp.concatenate([first, move(first, ALONG_X)])
    second = jnp.concatenate([second, move(second, ALONG_Y)])
    first_chips += shift(first_chips, 1)
    second_chips += shift(second_chips, 2)
    held = [
        (first, first_chips),
        (second, second_chips),
        (move(first, ALONG_Y), shift(first_chips, 2)),
        (move(second, ALONG_X), shift(second_chips, 1)),
    ]
    arrays = [a for a, _ in held] + [move(a, CORE) for a, _ in held]
    meta = tuple((c, False) for _, c in held) + tuple((c, True) for _, c in held)
    return arrays, meta


def scatter_group(keep, send):
    move = lambda v, mask: swap(v, mask, SLABS)
    wide = lambda v: v.astype(f32)
    shape = (Z_COUNT, 2, 2) + keep.shape[1:]
    got = move(send, CORE).reshape(shape)
    keep = keep.reshape(shape)
    chip = lambda z, y, x: wide(keep[z, y, x]) + wide(got[z, y, x])
    low, high = slice(0, 2), slice(2, 4)
    every = slice(None)
    first = move(chip(low, 1, every).astype(bf16), ALONG_Y)
    second = move(chip(high, every, 1).astype(bf16), ALONG_X)
    first_sum = lambda x: chip(low, 0, x) + wide(first[:, x])
    second_sum = lambda y: chip(high, y, 0) + wide(second[:, y])
    first_more = move(first_sum(1).astype(bf16), ALONG_X)
    second_more = move(second_sum(1).astype(bf16), ALONG_Y)
    low_part = first_sum(0) + wide(first_more)
    high_part = second_sum(0) + wide(second_more)
    parts = [low_part[0], low_part[1], high_part[0], high_part[1]]
    total = parts[0]
    for k in range(1, Z_COUNT):
        total = total + wide(move(parts[k].astype(bf16), k * ALONG_Z))
    return total


def gather_fast(shards, linear):
    (qw, kw, vw, ow, qb, vb, ob, fg, fs, iw, ib, dw, db, sg, ss) = shards
    core = linear & 1
    vectors = jnp.pad(jnp.stack([qb, vb, ob, fg, fs, db, sg, ss], axis=1), ((0, 0), (0, 120)))
    inner_bias = jnp.pad(ib.reshape(1, 4 * SLAB), ((0, SLAB - 1), (0, 128 - 4 * SLAB)))
    half = D // 2
    halves = [
        jnp.concatenate([qw, kw[:, :half], vectors, ow[:, :half], iw[:, :INNER_HALF]], axis=1),
        jnp.concatenate([kw[:, half:], vw, inner_bias, ow[:, half:], iw[:, INNER_HALF:]], axis=1),
    ]
    low_core = core == 0
    own = jnp.where(low_core, halves[0], halves[1])
    other = swap(jnp.where(low_core, halves[1], halves[0]), CORE, SLABS)
    rows = jnp.concatenate([jnp.where(low_core, own, other), jnp.where(low_core, other, own)], axis=0)
    qkv_block = rows[:, :QKV_BLOCK]
    ffn_block = jnp.concatenate([rows[:, QKV_BLOCK:], dw[:PAIR_ROWS], dw[PAIR_ROWS:]], axis=1)
    return gather_group(qkv_block), gather_group(ffn_block)


def gather_plain(shards):
    (qw, kw, vw, ow, qb, vb, ob, fg, fs, iw, ib, dw, db, sg, ss) = [
        lax.all_gather(v, AXES, axis=0, tiled=True) for v in shards
    ]
    vectors = jnp.pad(jnp.stack([qb, vb, ob, fg, fs, db, sg, ss], axis=1), ((0, 0), (0, 120)))
    inner_bias = jnp.pad(ib.reshape(SLABS, 1, 4 * SLAB), ((0, 0), (0, SLAB - 1), (0, 128 - 4 * SLAB))).reshape(D, 128)
    half = D // 2
    chips = lambda v: v.reshape(CHIPS, PAIR_ROWS, -1)
    down = dw.reshape(CHIPS, 2, 2, PAIR_ROWS, D)
    first = [
        chips(jnp.concatenate([qw, kw[:, :half], vectors], axis=1)),
        chips(jnp.concatenate([kw[:, half:], vw, inner_bias], axis=1)),
    ]
    second = [
        jnp.concatenate(
            [
                chips(ow[:, c * half : (c + 1) * half]),
                chips(iw[:, c * INNER_HALF : (c + 1) * INNER_HALF]),
                down[:, c, 0],
                down[:, c, 1],
            ],
            axis=2,
        )
        for c in range(2)
    ]
    meta = ((tuple(range(CHIPS)), False), (tuple(range(CHIPS)), True))
    return (first, meta), (second, meta)


def local(fast, inputs, lengths, *rest):
    shards, cotangent = rest[:15], rest[15]
    if fast:
        linear = lax.axis_index(AXES)
        place = jnp.stack([linear >> 1, linear & 1]).astype(jnp.int32)
        (first, first_meta), (second, second_meta) = gather_fast(shards, linear)
    else:
        place = jnp.zeros((2,), jnp.int32)
        (first, first_meta), (second, second_meta) = gather_plain(shards)
    qkv, attended, stats, weights, vectors = attend(place, lengths, inputs, first, first_meta)
    inner_bias = weights[::SLAB, QKV_BLOCK + QKV_HALF : QKV_BLOCK + QKV_HALF + 4 * SLAB].reshape(1, FF).astype(f32)
    output, first_back, back, small, db1, ffn_keep, ffn_send = feed_forward(
        place, inputs, attended, cotangent, vectors, inner_bias, second, second_meta
    )
    grads, qkv_keep, qkv_send = attend_back(place, lengths, inputs, qkv, back, stats, small, db1)
    grad_input = input_back(first_back, grads, weights)
    if fast:
        ffn = scatter_group(ffn_keep, ffn_send)[None]
        proj = scatter_group(qkv_keep, qkv_send)[None]
    else:
        ffn, proj = (
            jnp.stack(pair, axis=1).reshape((SLABS,) + pair[0].shape[1:]).astype(f32)
            for pair in ((ffn_keep, ffn_send), (qkv_keep, qkv_send))
        )
    count = ffn.shape[0]
    shard = lambda v: v if fast else lax.psum_scatter(v, AXES, scatter_dimension=0, tiled=True)
    square = lambda i: shard(proj[:, SLAB * i : SLAB * (i + 1)].reshape(count * SLAB, D))
    tail = proj[:, 3 * SLAB :].reshape(count, 8, D // 128, 128)
    columns = jnp.swapaxes(tail[:, :, :3], 1, 2).reshape(count * SLAB, 128)
    vec = lambda i: shard(columns[:, i])
    inner_bias_grad = shard(tail[:, 0, 3, : 4 * SLAB].reshape(count * 4 * SLAB))
    down_grad = shard(ffn[:, : 4 * SLAB].reshape(count * 4 * SLAB, D))
    inner_grad = shard(
        jnp.swapaxes(ffn[:, 4 * SLAB : 8 * SLAB].reshape(count, 4, SLAB, D), 1, 2).reshape(count * SLAB, FF)
    )
    out_grad = shard(ffn[:, 8 * SLAB : 9 * SLAB].reshape(count * SLAB, D))
    return (
        output,
        grad_input,
        square(0),
        square(1),
        square(2),
        out_grad,
        vec(0),
        vec(1),
        vec(2),
        vec(3),
        vec(4),
        inner_grad,
        inner_bias_grad,
        down_grad,
        vec(5),
        vec(6),
        vec(7),
    )


def solution(mesh):
    rows, flat = P(AXES, None), P(AXES)
    params = (rows,) * 4 + (flat,) * 5 + (rows, flat, rows, flat, flat, flat)
    return jax.shard_map(
        functools.partial(local, dict(mesh.shape) == FAST_SHAPE),
        mesh=mesh,
        in_specs=(rows, flat) + params + (rows,),
        out_specs=(rows, rows) + params,
        check_vma=False,
    )
```

time: 1130 us -> 376 us (0.33); the launches traced: 1120 us -> 375 us
  waiting for transfers between devices: 721 us -> 160 us
  matrix products: 182 us -> 0 us
  Pallas kernels: 0 us -> 142 us
  blocking collectives: 82.9 us -> 0 us
  local copies, waits for them, and re-layouts: 75.7 us -> 14.7 us
  starting transfers between devices: 0.94 us -> 41.6 us
  other arithmetic: 37.9 us -> 15.8 us
  between operations: 15.4 us -> 0.98 us
    reduce_scatter x3 -> x0, waiting for transfers between devices: 283 us -> none  [the longest x1 142 us: settle_grads(): lax.psum_scatter(down_weight, ('dp', 'fsdp'), scatter_dimension=0, tiled=...]
    unnamed x15 -> x0, waiting for transfers between devices: 244 us -> none
    all_gather x6 -> x0, waiting for transfers between devices: 194 us -> none  [the longest x1 60.7 us: gather_first(): lax.all_gather(inner_weight, ('dp', 'fsdp'), axis=0, tiled=True)]
    dot_general x32 -> x0, matrix products: 182 us -> none  [the longest x6 72.1 us: product(): return jnp.dot(lhs_rows, rhs_cols, preferred_element_type=jnp.float32)]
    ppermute x0 -> x39, waiting for transfers between devices: none -> 160 us  [swap(): return lax.ppermute(v, AXES, [(i, i ^ mask) for i in range(count)])]
    pallas_call x0 -> x4, Pallas kernels: none -> 142 us  [the longest x1 74.7 us: feed_forward(): pl.pallas_call(functools.partial(ffn_kernel, meta, len(pieces), blocks),...]
    unnamed x2 -> x0, blocking collectives: 82.9 us -> none
    ppermute x0 -> x39, starting transfers between devices: none -> 41.6 us  [swap(): return lax.ppermute(v, AXES, [(i, i ^ mask) for i in range(count)])]
  transfers between devices with their start and end apart: 12 -> 39, of which waited for: 11 -> 18; matrix products, arithmetic and copies ran while one was open for 21% -> 5% of each run, Pallas kernels for 0% -> 18%
where the time goes in v1:
time: 376 us; the launch traced here: 375 us
  waiting for transfers between devices  160 us (43%)
  Pallas kernels  142 us (38%)
  starting transfers between devices  41.6 us (11%)
  other arithmetic  15.8 us (4%)
  local copies, waits for them, and re-layouts  14.7 us (4%)
    ppermute x39, waiting for transfers between devices, swap(): return lax.ppermute(v, AXES, [(i, i ^ mask) for i in range(count)])  160 us
    pallas_call x1, Pallas kernels, feed_forward(): pl.pallas_call(functools.partial(ffn_kernel, meta, len(pieces), blocks),...  74.7 us
    ppermute x39, starting transfers between devices, swap(): return lax.ppermute(v, AXES, [(i, i ^ mask) for i in range(count)])  41.6 us
    pallas_call x1, Pallas kernels, attend_back(): pl.pallas_call(functools.partial(attend_back_kernel, seqs), grid=(seqs *...  40.6 us
    pallas_call x1, Pallas kernels, attend(): pl.pallas_call(functools.partial(attend_kernel, meta, len(pieces)), grid=...  17.1 us
    pallas_call x1, Pallas kernels, input_back(): pl.pallas_call(input_back_kernel, grid=(count // BLOCK,), in_specs=[pl.Bl...  9.37 us
  transfers between devices with their start and end apart: 39, of which 18 were waited for; matrix products, arithmetic and copies ran while one was open for 5% of the time, Pallas kernels for 18%

profile of v1, /device:TPU:0, one launch (start us, length us, event | category | flops | bytes accessed | tf_op | source)
XLA Modules:
  0.0 375.1 jit_solution(17866272538743846310)
XLA Ops:
  7.8 3.0 collective-permute-start.12
  10.8 2.5 collective-permute-start.4
  13.6 1.7 collective-permute-start.1
  15.3 2.5 collective-permute-start.15
  17.8 6.9 %collective-permute-done.12 = bf16[48,3456]{1,0:T(8,128)(2,1)S(1)} collective-permute-done((bf16[48,3456]{1,0:T(8,128)(2,1)S(1)}, bf16[48,3456]{1,0:T(8,128)(2,1)S(1)}, u32[]{:S(2)}, u32[]{:S(2)}) %collective-permute-start.12) | collective-permute-done | bytes 331808 | tf_op jit(solution)/shard_map/ppermute | solution.py:563
  24.7 2.0 collective-permute-start.14
  26.8 10.3 %collective-permute-done.15 = bf16[48,3456]{1,0:T(8,128)(2,1)S(1)} collective-permute-done((bf16[48,3456]{1,0:T(8,128)(2,1)S(1)}, bf16[48,3456]{1,0:T(8,128)(2,1)S(1)}, u32[]{:S(2)}, u32[]{:S(2)}) %collective-permute-start.15) | collective-permute-done | bytes 331808 | tf_op jit(solution)/shard_map/ppermute | solution.py:563
  38.6 14.7 %collective-permute-done.14 = bf16[48,3456]{1,0:T(8,128)(2,1)S(1)} collective-permute-done((bf16[48,3456]{1,0:T(8,128)(2,1)S(1)}, bf16[48,3456]{1,0:T(8,128)(2,1)S(1)}, u32[]{:S(2)}, u32[]{:S(2)}) %collective-permute-start.14) | collective-permute-done | bytes 331808 | tf_op jit(solution)/shard_map/ppermute | solution.py:563
  57.2 14.0 %collective-permute-done.16 = bf16[2,48,3456]{2,1,0:T(8,128)(2,1)S(1)} collective-permute-done((bf16[2,48,3456]{2,1,0:T(8,128)(2,1)S(1)}, bf16[2,48,3456]{2,1,0:T(8,128)(2,1)S(1)}, u32[]{:S(2)}, u32[]{:S(2)}) %collective-permute-start.16) | collective-permute-done | bytes 663584 | tf_op jit(solution)/shard_map/ppermute | solution.py:563
  75.3 29.6 %collective-permute-done.5 = bf16[2,48,1280]{2,1,0:T(8,128)(2,1)S(1)} collective-permute-done((bf16[2,48,1280]{2,1,0:T(8,128)(2,1)S(1)}, bf16[2,48,1280]{2,1,0:T(8,128)(2,1)S(1)}, u32[]{:S(2)}, u32[]{:S(2)}) %collective-permute-start.5) | collective-permute-done | bytes 245792 | tf_op jit(solution)/shard_map/ppermute | solution.py:563
  106.6 6.8 %collective-permute-done.6.refs_2_ = bf16[4,48,1280]{2,1,0:T(8,128)(2,1)S(1)} collective-permute-done((bf16[4,48,1280]{2,1,0:T(8,128)(2,1)S(1)}, bf16[4,48,1280]{2,1,0:T(8,128)(2,1)S(1)}, u32[]{:S(2)}, u32[]{:S(2)}) %collective-permute-start.6) | collective-permute-done | bytes 491552 | tf_op jit(solution)/shard_map/ppermute | solution.py:563
  114.5 4.3 %collective-permute-done.7.refs_3_ = bf16[4,48,1280]{2,1,0:T(8,128)(2,1)} collective-permute-done((bf16[4,48,1280]{2,1,0:T(8,128)(2,1)S(1)}, bf16[4,48,1280]{2,1,0:T(8,128)(2,1)}, u32[]{:S(2)}, u32[]{:S(2)}) %collective-permute-start.7) | collective-permute-done | bytes 491552 | tf_op jit(solution)/shard_map/ppermute | solution.py:563
  118.8 2.9 collective-permute-done.10.refs_6_
  124.8 17.1 %attend.1 = (bf16[1024,2304]{1,0:T(8,128)(2,1)}, bf16[1024,768]{1,0:T(8,128)(2,1)}, f32[2,16,512]{2,1,0:T(8,128)}, bf16[768,2560]{1,0:T(8,128)(2,1)}, f32[16,768]{1,0:T(8,128)}) custom-call(s32[2]{0:T(128)} %pad_add_fusion.place, s32[2]{0:T(128)} %lengths.3, f32[1024,768]{1,0:T(8,128)} %x_ref.5, bf16[4,48,1280]{2,1,0:T(8,128)(2,1)} %copy-done.4, ...), custom_call_target="tpu_custom_call" | custom-call | flops 3623878656 | bytes 20971520 | tf_op jit(solution)/shard_map/attend/pallas_call | solution.py:172
  143.5 74.7 %feed_forward.1 = (f32[1024,768]{1,0:T(8,128)}, f32[1024,768]{1,0:T(8,128)}, bf16[1024,768]{1,0:T(8,128)(2,1)}, f32[8,768]{1,0:T(8,128)}, f32[1,3072]{1,0:T(1,12...) custom-call(s32[2]{0:T(128)} %pad_add_fusion.place, f32[1024,768]{1,0:T(8,128)} %x_ref.5, ...), custom_call_target="tpu_custom_call" | custom-call | flops 32614907904 | bytes 41943040 | tf_op jit(solution)/shard_map/feed_forward/pallas_call | solution.py:364
  218.4 40.6 %attend_back.1 = (bf16[1024,2304]{1,0:T(8,128)(2,1)}, bf16[16,80,768]{2,1,0:T(8,128)(2,1)}, bf16[16,80,768]{2,1,0:T(8,128)(2,1)}) custom-call(s32[2]{0:T(128)} %pad_add_fusion.place, s32[2]{0:T(128)} %lengths.3, f32[1024,768]{1,0:T(8,128)} %x_ref.5, bf16[1024,2304]{1,0:T(8,128)(2,1)} %get-tuple-element.37.qkv_ref, ...), custom_call_target="tpu_custom_call" | custom-call | flops 3623878656 | bytes 31457280 | tf_op jit(solution)/shard_map/attend_back/pallas_call | solution.py:499
  259.4 3.8 %collective-permute-done.23 = bf16[16,80,768]{2,1,0:T(8,128)(2,1)S(1)} collective-permute-done((bf16[16,80,768]{2,1,0:T(8,128)(2,1)}, bf16[16,80,768]{2,1,0:T(8,128)(2,1)S(1)}, u32[]{:S(2)}, u32[]{:S(2)}) %collective-permute-start.23) | collective-permute-done | bytes 1966112 | tf_op jit(solution)/shard_map/ppermute | solution.py:563
  268.9 9.2 %collective-permute-done.27 = bf16[2,2,80,768]{3,2,0,1:T(8,128)(2,1)S(1)} collective-permute-done((bf16[2,2,80,768]{3,2,0,1:T(8,128)(2,1)S(1)}, bf16[2,2,80,768]{3,2,0,1:T(8,128)(2,1)S(1)}, u32[]{:S(2)}, u32[]{:S(2)}) %collective-permute-start.27) | collective-permute-done | bytes 491552 | tf_op jit(solution)/shard_map/ppermute | solution.py:563
  279.8 1.7 fusion.1
  283.0 2.8 collective-permute-done.28
  286.7 2.5 collective-permute-start.30
  290.5 2.8 fusion
  294.9 23.2 %collective-permute-done.25 = bf16[2,80,768]{2,1,0:T(8,128)(2,1)S(1)} collective-permute-done((bf16[2,80,768]{2,1,0:T(8,128)(2,1)S(1)}, bf16[2,80,768]{2,1,0:T(8,128)(2,1)S(1)}, u32[]{:S(2)}, u32[]{:S(2)}) %collective-permute-start.25) | collective-permute-done | bytes 245792 | tf_op jit(solution)/shard_map/ppermute | solution.py:563
  318.9 2.3 fusion.2
  321.7 9.4 %input_back.1 = f32[1024,768]{1,0:T(8,128)} custom-call(f32[1024,768]{1,0:T(8,128)} %get-tuple-element.36.fb_ref, bf16[1024,2304]{1,0:T(8,128)(2,1)} %get-tuple-element.42.grads_ref, bf16[768,2560]{1,0:T(8,128)(2,1)} %get-tuple-element.34.w_ref), custom_call_target="tpu_custom_call" | custom-call | flops 3623878656 | bytes 15728640 | tf_op jit(solution)/shard_map/input_back/pallas_call | solution.py:543
  332.1 6.4 %collective-permute-done.36 = bf16[2,224,768]{2,1,0:T(8,128)(2,1)S(1)} collective-permute-done((bf16[2,224,768]{2,1,0:T(8,128)(2,1)}, bf16[2,224,768]{2,1,0:T(8,128)(2,1)S(1)}, u32[]{:S(2)}, u32[]{:S(2)}) %collective-permute-start.36) | collective-permute-done | bytes 688160 | tf_op jit(solution)/shard_map/ppermute | solution.py:563
  338.5 2.1 fusion.4
  342.0 2.2 collective-permute-start.37
  345.6 11.1 %collective-permute-done.33 = bf16[2,224,768]{2,1,0:T(8,128)(2,1)S(1)} collective-permute-done((bf16[2,224,768]{2,1,0:T(8,128)(2,1)S(1)}, bf16[2,224,768]{2,1,0:T(8,128)(2,1)S(1)}, u32[]{:S(2)}, u32[]{:S(2)}) %collective-permute-start.33) | collective-permute-done | bytes 688160 | tf_op jit(solution)/shard_map/ppermute | solution.py:563
  356.8 1.7 fusion.6
  360.1 5.4 %collective-permute-done.37 = bf16[224,768]{1,0:T(8,128)(2,1)S(1)} collective-permute-done((bf16[224,768]{1,0:T(8,128)(2,1)S(1)}, bf16[224,768]{1,0:T(8,128)(2,1)S(1)}, u32[]{:S(2)}, u32[]{:S(2)}) %collective-permute-start.37) | collective-permute-done | bytes 344096 | tf_op jit(solution)/shard_map/ppermute | solution.py:563
  365.4 7.2 %collective-permute-done.34 = bf16[224,768]{1,0:T(8,128)(2,1)S(1)} collective-permute-done((bf16[224,768]{1,0:T(8,128)(2,1)S(1)}, bf16[224,768]{1,0:T(8,128)(2,1)S(1)}, u32[]{:S(2)}, u32[]{:S(2)}) %collective-permute-start.34) | collective-permute-done | bytes 344096 | tf_op jit(solution)/shard_map/ppermute | solution.py:563
  (119 shorter events, 46.8 us)
Async XLA Ops:
  7.8 16.9 %collective-permute-start.12 = (bf16[48,3456]{1,0:T(8,128)(2,1)S(1)}, bf16[48,3456]{1,0:T(8,128)(2,1)S(1)}, u32[]{:S(2)}, u32[]{:S(2)}) collective-permute-start(bf16[48,3456]{1,0:T(8,128)(2,1)S(1)} %fusion.20), channel_id=1, source_target_pairs={{0,8},{1,9},{2,10},{3,11},{4,12},{5,13},{6,14},{7,15},{8,0},{9,1},... | collective-permute-start | bytes 995336 | tf_op jit(solution)/shard_map/ppermute | solution.py:563
  10.8 62.1 %collective-permute-start.4 = (bf16[48,1280]{1,0:T(8,128)(2,1)S(1)}, bf16[48,1280]{1,0:T(8,128)(2,1)S(1)}, u32[]{:S(2)}, u32[]{:S(2)}) collective-permute-start(bf16[48,1280]{1,0:T(8,128)(2,1)S(1)} %pad_maximum_fusion.9), channel_id=1, source_target_pairs={{0,24},{1,25},{2,26},{3,27},{4,28},{5,29},{6,30},{7,31},{8,16},{9,... | collective-permute-start | bytes 368648 | tf_op jit(solution)/shard_map/ppermute | solution.py:563
  13.4 59.6 %collective-permute-start.3 = (bf16[48,1280]{1,0:T(8,128)(2,1)S(1)}, bf16[48,1280]{1,0:T(8,128)(2,1)S(1)}, u32[]{:S(2)}, u32[]{:S(2)}) collective-permute-start(bf16[48,1280]{1,0:T(8,128)(2,1)S(1)} %pad_maximum_fusion.9), channel_id=1, source_target_pairs={{0,16},{1,17},{2,18},{3,19},{4,20},{5,21},{6,22},{7,23},{8,24},{9,... | collective-permute-start | bytes 368648 | tf_op jit(solution)/shard_map/ppermute | solution.py:563
  13.6 41.3 %collective-permute-start.1 = (bf16[48,1280]{1,0:T(8,128)(2,1)S(1)}, bf16[48,1280]{1,0:T(8,128)(2,1)S(1)}, u32[]{:S(2)}, u32[]{:S(2)}) collective-permute-start(bf16[48,1280]{1,0:T(8,128)(2,1)S(1)} %pad_maximum_fusion.9), channel_id=1, source_target_pairs={{0,8},{1,9},{2,10},{3,11},{4,12},{5,13},{6,14},{7,15},{8,0},{9,1},... | collective-permute-start | bytes 368648 | tf_op jit(solution)/shard_map/ppermute | solution.py:563
  15.3 21.8 %collective-permute-start.15 = (bf16[48,3456]{1,0:T(8,128)(2,1)S(1)}, bf16[48,3456]{1,0:T(8,128)(2,1)S(1)}, u32[]{:S(2)}, u32[]{:S(2)}) collective-permute-start(bf16[48,3456]{1,0:T(8,128)(2,1)S(1)} %fusion.20), channel_id=1, source_target_pairs={{0,24},{1,25},{2,26},{3,27},{4,28},{5,29},{6,30},{7,31},{8,16},{9,... | collective-permute-start | bytes 995336 | tf_op jit(solution)/shard_map/ppermute | solution.py:563
  24.7 28.6 %collective-permute-start.14 = (bf16[48,3456]{1,0:T(8,128)(2,1)S(1)}, bf16[48,3456]{1,0:T(8,128)(2,1)S(1)}, u32[]{:S(2)}, u32[]{:S(2)}) collective-permute-start(bf16[48,3456]{1,0:T(8,128)(2,1)S(1)} %fusion.20), channel_id=1, source_target_pairs={{0,16},{1,17},{2,18},{3,19},{4,20},{5,21},{6,22},{7,23},{8,24},{9,... | collective-permute-start | bytes 995336 | tf_op jit(solution)/shard_map/ppermute | solution.py:563
  37.1 19.4 %collective-permute-start.13 = (bf16[2,48,3456]{2,1,0:T(8,128)(2,1)S(1)}, bf16[2,48,3456]{2,1,0:T(8,128)(2,1)S(1)}, u32[]{:S(2)}, u32[]{:S(2)}) collective-permute-start(bf16[2,48,3456]{2,1,0:T(8,128)(2,1)S(1)} %pad_maximum_fusion.2), channel_id=1, source_target_pairs={{0,2},{1,3},{2,0},{3,1},{4,6},{5,7},{6,4},{7,5},{8,10},{9,11},{10,... | collective-permute-start | bytes 1990664 | tf_op jit(solution)/shard_map/ppermute | solution.py:563
  53.3 17.9 %collective-permute-start.16 = (bf16[2,48,3456]{2,1,0:T(8,128)(2,1)S(1)}, bf16[2,48,3456]{2,1,0:T(8,128)(2,1)S(1)}, u32[]{:S(2)}, u32[]{:S(2)}) collective-permute-start(bf16[2,48,3456]{2,1,0:T(8,128)(2,1)S(1)} %pad_maximum_fusion.3), channel_id=1, source_target_pairs={{0,4},{1,5},{2,6},{3,7},{4,0},{5,1},{6,2},{7,3},{8,12},{9,13},{10,... | collective-permute-start | bytes 1990664 | tf_op jit(solution)/shard_map/ppermute | solution.py:563
  54.9 19.6 %collective-permute-start.2 = (bf16[2,48,1280]{2,1,0:T(8,128)(2,1)S(1)}, bf16[2,48,1280]{2,1,0:T(8,128)(2,1)S(1)}, u32[]{:S(2)}, u32[]{:S(2)}) collective-permute-start(bf16[2,48,1280]{2,1,0:T(8,128)(2,1)S(1)} %pad_maximum_fusion.7), channel_id=1, source_target_pairs={{0,2},{1,3},{2,0},{3,1},{4,6},{5,7},{6,4},{7,5},{8,10},{9,11},{10,... | collective-permute-start | bytes 737288 | tf_op jit(solution)/shard_map/ppermute | solution.py:563
  56.7 57.4 %collective-permute-start.17 = (bf16[4,48,3456]{2,1,0:T(8,128)(2,1)S(1)}, bf16[4,48,3456]{2,1,0:T(8,128)(2,1)}, u32[]{:S(2)}, u32[]{:S(2)}) collective-permute-start(bf16[4,48,3456]{2,1,0:T(8,128)(2,1)S(1)} %pad_maximum_fusion.refs_0_), channel_id=1, source_target_pairs={{0,4},{1,5},{2,6},{3,7},{4,0},{5,1},{6,2},{7,3},{8,12},{9,13},{10,... | collective-permute-start | bytes 3981320 | tf_op jit(solution)/shard_map/ppermute | solution.py:563
  71.4 42.7 %collective-permute-start.18 = (bf16[4,48,3456]{2,1,0:T(8,128)(2,1)S(1)}, bf16[4,48,3456]{2,1,0:T(8,128)(2,1)}, u32[]{:S(2)}, u32[]{:S(2)}) collective-permute-start(bf16[4,48,3456]{2,1,0:T(8,128)(2,1)S(1)} %pad_maximum_fusion.1.refs_1_), channel_id=1, source_target_pairs={{0,2},{1,3},{2,0},{3,1},{4,6},{5,7},{6,4},{7,5},{8,10},{9,11},{10,... | collective-permute-start | bytes 3981320 | tf_op jit(solution)/shard_map/ppermute | solution.py:563
  73.0 31.9 %collective-permute-start.5 = (bf16[2,48,1280]{2,1,0:T(8,128)(2,1)S(1)}, bf16[2,48,1280]{2,1,0:T(8,128)(2,1)S(1)}, u32[]{:S(2)}, u32[]{:S(2)}) collective-permute-start(bf16[2,48,1280]{2,1,0:T(8,128)(2,1)S(1)} %pad_maximum_fusion.8), channel_id=1, source_target_pairs={{0,4},{1,5},{2,6},{3,7},{4,0},{5,1},{6,2},{7,3},{8,12},{9,13},{10,... | collective-permute-start | bytes 737288 | tf_op jit(solution)/shard_map/ppermute | solution.py:563
  74.6 30.4 %collective-permute-start.8 = (bf16[4,48,1280]{2,1,0:T(8,128)(2,1)S(1)}, bf16[4,48,1280]{2,1,0:T(8,128)(2,1)S(1)}, u32[]{:S(2)}, u32[]{:S(2)}) collective-permute-start(bf16[4,48,1280]{2,1,0:T(8,128)(2,1)S(1)} %pad_maximum_fusion.4.refs_0_), channel_id=1, source_target_pairs={{0,1},{1,0},{2,3},{3,2},{4,5},{5,4},{6,7},{7,6},{8,9},{9,8},{10,11... | collective-permute-start | bytes 1474568 | tf_op jit(solution)/shard_map/ppermute | solution.py:563
  74.7 38.8 %collective-permute-start.6 = (bf16[4,48,1280]{2,1,0:T(8,128)(2,1)S(1)}, bf16[4,48,1280]{2,1,0:T(8,128)(2,1)S(1)}, u32[]{:S(2)}, u32[]{:S(2)}) collective-permute-start(bf16[4,48,1280]{2,1,0:T(8,128)(2,1)S(1)} %pad_maximum_fusion.4.refs_0_), channel_id=1, source_target_pairs={{0,4},{1,5},{2,6},{3,7},{4,0},{5,1},{6,2},{7,3},{8,12},{9,13},{10,... | collective-permute-start | bytes 1474568 | tf_op jit(solution)/shard_map/ppermute | solution.py:563
  105.1 13.7 %collective-permute-start.7 = (bf16[4,48,1280]{2,1,0:T(8,128)(2,1)S(1)}, bf16[4,48,1280]{2,1,0:T(8,128)(2,1)}, u32[]{:S(2)}, u32[]{:S(2)}) collective-permute-start(bf16[4,48,1280]{2,1,0:T(8,128)(2,1)S(1)} %pad_maximum_fusion.5.refs_1_), channel_id=1, source_target_pairs={{0,2},{1,3},{2,0},{3,1},{4,6},{5,7},{6,4},{7,5},{8,10},{9,11},{10,... | collective-permute-start | bytes 1474568 | tf_op jit(solution)/shard_map/ppermute | solution.py:563
  113.5 30.0 %collective-permute-start.19 = (bf16[4,48,3456]{2,1,0:T(8,128)(2,1)S(1)}, bf16[4,48,3456]{2,1,0:T(8,128)(2,1)}, u32[]{:S(2)}, u32[]{:S(2)}) collective-permute-start(bf16[4,48,3456]{2,1,0:T(8,128)(2,1)S(1)} %pad_maximum_fusion.refs_0_), channel_id=1, source_target_pairs={{0,1},{1,0},{2,3},{3,2},{4,5},{5,4},{6,7},{7,6},{8,9},{9,8},{10,11... | collective-permute-start | bytes 3981320 | tf_op jit(solution)/shard_map/ppermute | solution.py:563
  113.5 30.0 %collective-permute-start.20 = (bf16[4,48,3456]{2,1,0:T(8,128)(2,1)S(1)}, bf16[4,48,3456]{2,1,0:T(8,128)(2,1)}, u32[]{:S(2)}, u32[]{:S(2)}) collective-permute-start(bf16[4,48,3456]{2,1,0:T(8,128)(2,1)S(1)} %pad_maximum_fusion.1.refs_1_), channel_id=1, source_target_pairs={{0,1},{1,0},{2,3},{3,2},{4,5},{5,4},{6,7},{7,6},{8,9},{9,8},{10,11... | collective-permute-start | bytes 3981320 | tf_op jit(solution)/shard_map/ppermute | solution.py:563
  114.0 29.5 %collective-permute-start.21 = (bf16[4,48,3456]{2,1,0:T(8,128)(2,1)}, bf16[4,48,3456]{2,1,0:T(8,128)(2,1)}, u32[]{:S(2)}, u32[]{:S(2)}) collective-permute-start(bf16[4,48,3456]{2,1,0:T(8,128)(2,1)} %collective-permute-done.17.refs_2_), channel_id=1, source_target_pairs={{0,1},{1,0},{2,3},{3,2},{4,5},{5,4},{6,7},{7,6},{8,9},{9,8},{10,11... | collective-permute-start | bytes 3981320 | tf_op jit(solution)/shard_map/ppermute | solution.py:563
  114.1 29.4 %collective-permute-start.22 = (bf16[4,48,3456]{2,1,0:T(8,128)(2,1)}, bf16[4,48,3456]{2,1,0:T(8,128)(2,1)}, u32[]{:S(2)}, u32[]{:S(2)}) collective-permute-start(bf16[4,48,3456]{2,1,0:T(8,128)(2,1)} %collective-permute-done.18.refs_3_), channel_id=1, source_target_pairs={{0,1},{1,0},{2,3},{3,2},{4,5},{5,4},{6,7},{7,6},{8,9},{9,8},{10,11... | collective-permute-start | bytes 3981320 | tf_op jit(solution)/shard_map/ppermute | solution.py:563
  218.2 61.6 %collective-permute-start.31 = (bf16[16,224,768]{2,1,0:T(8,128)(2,1)}, bf16[16,224,768]{2,1,0:T(8,128)(2,1)}, u32[]{:S(2)}, u32[]{:S(2)}) collective-permute-start(bf16[16,224,768]{2,1,0:T(8,128)(2,1)} %get-tuple-element.46), channel_id=1, source_target_pairs={{0,1},{1,0},{2,3},{3,2},{4,5},{5,4},{6,7},{7,6},{8,9},{9,8},{10,11... | collective-permute-start | bytes 16515080 | tf_op jit(solution)/shard_map/ppermute | solution.py:563
  264.5 13.6 %collective-permute-start.27 = (bf16[2,2,80,768]{3,2,0,1:T(8,128)(2,1)S(1)}, bf16[2,2,80,768]{3,2,0,1:T(8,128)(2,1)S(1)}, u32[]{:S(2)}, u32[]{:S(2)}) collective-permute-start(bf16[2,2,80,768]{3,2,0,1:T(8,128)(2,1)S(1)} %fusion.12), channel_id=1, source_target_pairs={{0,2},{1,3},{2,0},{3,1},{4,6},{5,7},{6,4},{7,5},{8,10},{9,11},{10,... | collective-permute-start | bytes 1474568 | tf_op jit(solution)/shard_map/ppermute | solution.py:563
  267.3 15.8 %collective-permute-start.24 = (bf16[2,2,80,768]{3,2,0,1:T(8,128)(2,1)S(1)}, bf16[2,2,80,768]{3,2,0,1:T(8,128)(2,1)S(1)}, u32[]{:S(2)}, u32[]{:S(2)}) collective-permute-start(bf16[2,2,80,768]{3,2,0,1:T(8,128)(2,1)S(1)} %fusion.11), channel_id=1, source_target_pairs={{0,4},{1,5},{2,6},{3,7},{4,0},{5,1},{6,2},{7,3},{8,12},{9,13},{10,... | collective-permute-start | bytes 1474568 | tf_op jit(solution)/shard_map/ppermute | solution.py:563
  281.5 37.5 %collective-permute-start.35 = (bf16[2,2,224,768]{3,2,0,1:T(8,128)(2,1)S(1)}, bf16[2,2,224,768]{3,2,0,1:T(8,128)(2,1)S(1)}, u32[]{:S(2)}, u32[]{:S(2)}) collective-permute-start(bf16[2,2,224,768]{3,2,0,1:T(8,128)(2,1)S(1)} %fusion.1), channel_id=1, source_target_pairs={{0,2},{1,3},{2,0},{3,1},{4,6},{5,7},{6,4},{7,5},{8,10},{9,11},{10,... | collective-permute-start | bytes 4128776 | tf_op jit(solution)/shard_map/ppermute | solution.py:563
  286.7 44.3 %collective-permute-start.29 = (bf16[80,768]{1,0:T(8,128)(2,1)}, bf16[80,768]{1,0:T(8,128)(2,1)S(1)}, u32[]{:S(2)}, u32[]{:S(2)}) collective-permute-start(bf16[80,768]{1,0:T(8,128)(2,1)} %get-tuple-element.68), channel_id=1, source_target_pairs={{0,16},{1,17},{2,18},{3,19},{4,20},{5,21},{6,22},{7,23},{8,24},{9,... | collective-permute-start | bytes 368648 | tf_op jit(solution)/shard_map/ppermute | solution.py:563
  286.7 44.3 %collective-permute-start.30 = (bf16[80,768]{1,0:T(8,128)(2,1)}, bf16[80,768]{1,0:T(8,128)(2,1)S(1)}, u32[]{:S(2)}, u32[]{:S(2)}) collective-permute-start(bf16[80,768]{1,0:T(8,128)(2,1)} %get-tuple-element.69), channel_id=1, source_target_pairs={{0,24},{1,25},{2,26},{3,27},{4,28},{5,29},{6,30},{7,31},{8,16},{9,... | collective-permute-start | bytes 368648 | tf_op jit(solution)/shard_map/ppermute | solution.py:563
  289.2 29.0 %collective-permute-start.25 = (bf16[2,80,768]{2,1,0:T(8,128)(2,1)S(1)}, bf16[2,80,768]{2,1,0:T(8,128)(2,1)S(1)}, u32[]{:S(2)}, u32[]{:S(2)}) collective-permute-start(bf16[2,80,768]{2,1,0:T(8,128)(2,1)S(1)} %get-tuple-element.58), channel_id=1, source_target_pairs={{0,2},{1,3},{2,0},{3,1},{4,6},{5,7},{6,4},{7,5},{8,10},{9,11},{10,... | collective-permute-start | bytes 737288 | tf_op jit(solution)/shard_map/ppermute | solution.py:563
  293.4 38.7 %collective-permute-start.32 = (bf16[2,2,224,768]{3,2,0,1:T(8,128)(2,1)}, bf16[2,2,224,768]{3,2,0,1:T(8,128)(2,1)}, u32[]{:S(2)}, u32[]{:S(2)}) collective-permute-start(bf16[2,2,224,768]{3,2,0,1:T(8,128)(2,1)} %fusion), channel_id=1, source_target_pairs={{0,4},{1,5},{2,6},{3,7},{4,0},{5,1},{6,2},{7,3},{8,12},{9,13},{10,... | collective-permute-start | bytes 4128776 | tf_op jit(solution)/shard_map/ppermute | solution.py:563
  321.2 17.3 %collective-permute-start.36 = (bf16[2,224,768]{2,1,0:T(8,128)(2,1)}, bf16[2,224,768]{2,1,0:T(8,128)(2,1)S(1)}, u32[]{:S(2)}, u32[]{:S(2)}) collective-permute-start(bf16[2,224,768]{2,1,0:T(8,128)(2,1)} %fusion.2), channel_id=1, source_target_pairs={{0,4},{1,5},{2,6},{3,7},{4,0},{5,1},{6,2},{7,3},{8,12},{9,13},{10,... | collective-permute-start | bytes 2064392 | tf_op jit(solution)/shard_map/ppermute | solution.py:563
  340.6 16.2 %collective-permute-start.33 = (bf16[2,224,768]{2,1,0:T(8,128)(2,1)S(1)}, bf16[2,224,768]{2,1,0:T(8,128)(2,1)S(1)}, u32[]{:S(2)}, u32[]{:S(2)}) collective-permute-start(bf16[2,224,768]{2,1,0:T(8,128)(2,1)S(1)} %get-tuple-element.56), channel_id=1, source_target_pairs={{0,2},{1,3},{2,0},{3,1},{4,6},{5,7},{6,4},{7,5},{8,10},{9,11},{10,... | collective-permute-start | bytes 2064392 | tf_op jit(solution)/shard_map/ppermute | solution.py:563
  342.0 23.4 %collective-permute-start.37 = (bf16[224,768]{1,0:T(8,128)(2,1)S(1)}, bf16[224,768]{1,0:T(8,128)(2,1)S(1)}, u32[]{:S(2)}, u32[]{:S(2)}) collective-permute-start(bf16[224,768]{1,0:T(8,128)(2,1)S(1)} %get-tuple-element.61), channel_id=1, source_target_pairs={{0,16},{1,17},{2,18},{3,19},{4,20},{5,21},{6,22},{7,23},{8,24},{9,... | collective-permute-start | bytes 1032200 | tf_op jit(solution)/shard_map/ppermute | solution.py:563
  344.2 21.2 %collective-permute-start.38 = (bf16[224,768]{1,0:T(8,128)(2,1)S(1)}, bf16[224,768]{1,0:T(8,128)(2,1)S(1)}, u32[]{:S(2)}, u32[]{:S(2)}) collective-permute-start(bf16[224,768]{1,0:T(8,128)(2,1)S(1)} %get-tuple-element.62), channel_id=1, source_target_pairs={{0,24},{1,25},{2,26},{3,27},{4,28},{5,29},{6,30},{7,31},{8,16},{9,... | collective-permute-start | bytes 1032200 | tf_op jit(solution)/shard_map/ppermute | solution.py:563
  358.5 14.2 %collective-permute-start.34 = (bf16[224,768]{1,0:T(8,128)(2,1)S(1)}, bf16[224,768]{1,0:T(8,128)(2,1)S(1)}, u32[]{:S(2)}, u32[]{:S(2)}) collective-permute-start(bf16[224,768]{1,0:T(8,128)(2,1)S(1)} %fusion.18), channel_id=1, source_target_pairs={{0,8},{1,9},{2,10},{3,11},{4,12},{5,13},{6,14},{7,15},{8,0},{9,1},... | collective-permute-start | bytes 1032200 | tf_op jit(solution)/shard_map/ppermute | solution.py:563
  (17 other events, 330.1 us)

commit v2 on v1

v2 whole, which is shorter than its diff:
```python
import functools
import math

import jax
import jax.numpy as jnp
from jax import lax
from jax.experimental import pallas as pl
from jax.experimental.pallas import tpu as pltpu
from jax.sharding import PartitionSpec as P

D = 768
H = 12
DH = 64
FF = 3072
SLABS = 32
SLAB = D // SLABS
CHIPS = SLABS // 2
PAIR_ROWS = 2 * SLAB
NORM_EPSILON = 1e-12
MASKED_SCORE = -1000000000.0
GAUSS_DENSITY = 0.3989422804014327
LOG2E = 1.4426950408889634
MIB = 1 << 20

QKV_HALF = 3 * D // 2
QKV_BLOCK = QKV_HALF + 128
OUT_HALF = D // 2
INNER_HALF = FF // 2
FFN_BLOCK = OUT_HALF + INNER_HALF + 2 * D

bf16 = jnp.bfloat16
f32 = jnp.float32
ANY = pl.BlockSpec(memory_space=pl.ANY)
SMEM = pl.BlockSpec(memory_space=pltpu.SMEM)


def dot(a, b):
    return lax.dot_general(a, b, (((1,), (0,)), ((), ())), preferred_element_type=f32)


def dot_t(a, b):
    return lax.dot_general(a, b, (((1,), (1,)), ((), ())), preferred_element_type=f32)


def dot_l(a, b):
    return lax.dot_general(a, b, (((0,), (0,)), ((), ())), preferred_element_type=f32)


def aligned(start, size, unit):
    return pl.ds(pl.multiple_of(start, unit), size)


def qkv_blocks(place, pieces, weights, sem):
    chip, core = place[0], place[1]
    for ref, chips, other in pieces:
        half = 1 - core if other else core
        for slot, rel in enumerate(chips):
            rows = aligned((chip ^ rel) * PAIR_ROWS, PAIR_ROWS, 16)
            yield pltpu.make_async_copy(
                ref.at[slot], weights.at[rows, aligned(half * QKV_BLOCK, QKV_BLOCK, 128)], sem
            )


def ffn_blocks(place, pieces, out_w, inner_w, down_w, sem):
    chip, core = place[0], place[1]
    for ref, chips, other in pieces:
        half = 1 - core if other else core
        for slot, rel in enumerate(chips):
            owner = chip ^ rel
            rows = aligned(owner * PAIR_ROWS, PAIR_ROWS, 16)
            start = OUT_HALF + INNER_HALF
            yield pltpu.make_async_copy(
                ref.at[slot, :, pl.ds(0, OUT_HALF)],
                out_w.at[rows, aligned(half * OUT_HALF, OUT_HALF, 128)],
                sem.at[0],
            )
            yield pltpu.make_async_copy(
                ref.at[slot, :, pl.ds(OUT_HALF, INNER_HALF)],
                inner_w.at[rows, aligned(half * INNER_HALF, INNER_HALF, 128)],
                sem.at[1],
            )
            for i in range(2):
                down_rows = (owner * 2 + half) * (2 * PAIR_ROWS) + i * PAIR_ROWS
                yield pltpu.make_async_copy(
                    ref.at[slot, :, pl.ds(start + i * D, D)],
                    down_w.at[aligned(down_rows, PAIR_ROWS, 16), :],
                    sem.at[2],
                )


def hand_over(place, chip, half, keep, send, pairs, sem):
    slot = chip ^ place[0]
    for mine, out in ((True, keep), (False, send)):

        @pl.when((place[1] == half) == mine)
        def _():
            for source, lanes in pairs:
                pltpu.make_async_copy(source, out.at[slot, :, lanes], sem).start()


def wait_whole(ref, sem):
    pltpu.make_async_copy(ref, ref, sem).wait()


def lane_masks():
    low = (lax.broadcasted_iota(jnp.int32, (1, 128), 1) < DH).astype(f32)
    return low.astype(bf16), (1.0 - low).astype(bf16)


def attend_kernel(meta, n_pieces, place, lengths, x_ref, *refs):
    piece_refs = refs[:n_pieces]
    qkv_ref, att_ref, stat_ref, weights, vectors = refs[n_pieces : n_pieces + 5]
    sem = refs[-1]
    seq = pl.program_id(0)
    rows = x_ref.shape[0]

    @pl.when(seq == 0)
    def _():
        copies = list(qkv_blocks(place, [(r,) + m for r, m in zip(piece_refs, meta)], weights, sem))
        for c in copies:
            c.start()
        for c in copies:
            c.wait()
        small = weights[:, QKV_HALF:QKV_BLOCK].astype(f32)
        vectors[...] = small.T[0:16, :]

    lowered = x_ref[...].astype(bf16)
    first = dot(lowered, weights[:, 0:QKV_HALF])
    qkv_ref[:, 0:D] = (first[:, 0:D] + vectors[0:1, :]).astype(bf16)
    qkv_ref[:, D:QKV_HALF] = first[:, D:QKV_HALF].astype(bf16)
    second = dot(lowered, weights[:, QKV_BLOCK : QKV_BLOCK + QKV_HALF])
    qkv_ref[:, QKV_HALF : 2 * D] = second[:, 0 : D // 2].astype(bf16)
    qkv_ref[:, 2 * D :] = (second[:, D // 2 :] + vectors[1:2, :]).astype(bf16)

    low, high = lane_masks()
    lane = lax.broadcasted_iota(jnp.int32, (1, 128), 1)
    key_at = lax.broadcasted_iota(jnp.int32, (1, rows), 1)
    hidden_keys = jnp.where(key_at < lengths[seq], 0.0, MASKED_SCORE).astype(f32)
    chunk = 256
    ones = jnp.ones((rows, 128), bf16)
    stats = [jnp.zeros((chunk, 128), f32) for _ in range(rows // chunk)]
    for pair in range(H // 2):
        at = pair * 128
        keys = qkv_ref[:, D + at : D + at + 128]
        values = jnp.concatenate([qkv_ref[:, 2 * D + at : 2 * D + at + 128], ones], axis=1)
        keys_of = (keys * low, keys * high)
        for c in range(rows // chunk):
            span = pl.ds(c * chunk, chunk)
            queries = qkv_ref[span, at : at + 128]
            outs = []
            for i in range(2):
                scores = dot_t(queries, keys_of[i]) * (0.125 * LOG2E) + hidden_keys
                peak = jnp.max(scores, axis=-1, keepdims=True)
                weight = jnp.exp2(scores - peak).astype(bf16)
                both = dot(weight, values)
                total = both[:, 128:]
                outs.append(both[:, :128] / total)
                log_total = peak + jnp.log2(total)
                stats[c] = jnp.where(lane == 2 * pair + i, log_total, stats[c])
            att_ref[span, at : at + 128] = jnp.where(lane < DH, outs[0], outs[1]).astype(bf16)
    for c in range(rows // chunk):
        stat_ref[0, :, c * chunk : (c + 1) * chunk] = stats[c].T[0:16, :]


def attend(place, lengths, x, pieces, meta):
    rows = x.shape[0] // lengths.shape[0]
    seqs = lengths.shape[0]
    whole = lambda *shape: pl.BlockSpec(shape, lambda s: (0,) * len(shape))
    return pl.pallas_call(
        functools.partial(attend_kernel, meta, len(pieces)),
        grid=(seqs,),
        in_specs=[SMEM, SMEM, pl.BlockSpec((rows, D), lambda s: (s, 0))] + [ANY] * len(pieces),
        out_specs=[
            pl.BlockSpec((rows, 3 * D), lambda s: (s, 0)),
            pl.BlockSpec((rows, D), lambda s: (s, 0)),
            pl.BlockSpec((1, 16, rows), lambda s: (s, 0, 0)),
            whole(D, 2 * QKV_BLOCK),
            whole(16, D),
        ],
        out_shape=[
            jax.ShapeDtypeStruct((seqs * rows, 3 * D), bf16),
            jax.ShapeDtypeStruct((seqs * rows, D), bf16),
            jax.ShapeDtypeStruct((seqs, 16, rows), f32),
            jax.ShapeDtypeStruct((D, 2 * QKV_BLOCK), bf16),
            jax.ShapeDtypeStruct((16, D), f32),
        ],
        scratch_shapes=[pltpu.SemaphoreType.DMA],
        compiler_params=pltpu.CompilerParams(vmem_limit_bytes=56 * MIB),
        cost_estimate=pl.CostEstimate(flops=18_000_000_000, bytes_accessed=20 * MIB, transcendentals=0),
        name="attend",
    )(place, lengths, x, *pieces)


def gelu_parts(u):
    size = jnp.abs(u)
    bell = jnp.exp2(u * u * (-0.5 * LOG2E))
    t = 1.0 / (1.0 + (0.3275911 * math.sqrt(0.5)) * size)
    poly = t * (0.127414796 + t * (-0.142248368 + t * (0.7107068705 + t * (-0.7265760135 + t * 0.5307027145))))
    tail = poly * bell
    below = jnp.where(u < 0.0, tail, 1.0 - tail)
    return below, bell


def mean_rows(v):
    return jnp.sum(v, axis=-1, keepdims=True) * (1.0 / D)


def norm_rows(total):
    center = total - mean_rows(total)
    rstd = lax.rsqrt(mean_rows(center * center) + NORM_EPSILON)
    return center * rstd, rstd


def norm_back(upstream, normed, rstd, gain):
    scaled = upstream * gain
    return rstd * (scaled - mean_rows(scaled) - normed * mean_rows(scaled * normed))


BLOCK = 256
DOWN_STEPS = 8
INNER_STEPS = 4


def ffn_kernel(meta, n_pieces, blocks, place, x_ref, att_ref, cot_ref, vec_ref, b1_ref, *refs):
    piece_refs = refs[:n_pieces]
    (out_ref, fb_ref, ab_ref, small_ref, db1_ref, keep, send) = refs[n_pieces : n_pieces + 7]
    (out_w, inner_w, down_w, act, inner_back, hid, down_back, att, branch, slope, sem, wsem) = refs[
        n_pieces + 7 :
    ]
    step = pl.program_id(0)
    down_at, inner_at, out_at = blocks, blocks + DOWN_STEPS, blocks + DOWN_STEPS + INNER_STEPS

    @pl.when(step == 0)
    def _():
        copies = list(ffn_blocks(place, [(r,) + m for r, m in zip(piece_refs, meta)], out_w, inner_w, down_w, sem))
        for c in copies:
            c.start()
        small_ref[...] = jnp.zeros_like(small_ref)
        db1_ref[...] = jnp.zeros_like(db1_ref)

    @pl.when(step < blocks)
    def _():
        rows = aligned(step * BLOCK, BLOCK, BLOCK)

        @pl.when(step == 0)
        def _():
            wait_whole(out_w, sem.at[0])

        attended = att_ref[...]
        att[rows, :] = attended
        first_gain, first_shift = vec_ref[3:4, :], vec_ref[4:5, :]
        second_gain, second_shift = vec_ref[6:7, :], vec_ref[7:8, :]
        first_normed, first_rstd = norm_rows(x_ref[...] + dot(attended, out_w[...]) + vec_ref[2:3, :])
        hidden = first_normed * first_gain + first_shift
        hidden_low = hidden.astype(bf16)
        hid[rows, :] = hidden_low
        total = hidden + vec_ref[5:6, :]

        @pl.when(step == 0)
        def _():
            wait_whole(inner_w, sem.at[1])
            wait_whole(down_w, sem.at[2])

        for c in range(FF // D):
            cols = pl.ds(c * D, D)
            u = dot(hidden_low, inner_w[:, cols]) + b1_ref[:, cols]
            below, bell = gelu_parts(u)
            active = (u * below).astype(bf16)
            act[rows, cols] = active
            slope[:, cols] = below + u * bell * GAUSS_DENSITY
            total = total + dot(active, down_w[cols, :])
        second_normed, second_rstd = norm_rows(total)
        out_ref[...] = second_normed * second_gain + second_shift
        cot = cot_ref[...]
        second_back = norm_back(cot, second_normed, second_rstd, second_gain)
        back_low = second_back.astype(bf16)
        down_back[rows, :] = back_low
        hidden_back = second_back
        for c in range(FF // D):
            cols = pl.ds(c * D, D)
            ib = (dot_t(back_low, down_w[cols, :]) * slope[:, cols]).astype(bf16)
            inner_back[rows, cols] = ib
            db1_ref[:, cols] += jnp.sum(ib.astype(f32), axis=0, keepdims=True)
            hidden_back = hidden_back + dot_t(ib, inner_w[:, cols])
        first_back = norm_back(hidden_back, first_normed, first_rstd, first_gain)
        fb_ref[...] = first_back
        branch_low = first_back.astype(bf16)
        branch[rows, :] = branch_low
        ab_ref[...] = dot_t(branch_low, out_w[...]).astype(bf16)
        sums = (
            branch_low.astype(f32),
            hidden_back * first_normed,
            hidden_back,
            back_low.astype(f32),
            cot * second_normed,
            cot,
        )
        for i, v in enumerate(sums):
            small_ref[2 + i : 3 + i, :] += jnp.sum(v, axis=0, keepdims=True)

    @pl.when((step >= down_at) & (step < inner_at))
    def _():
        chunk = step - down_at
        width = FF // DOWN_STEPS
        rows = aligned(chunk * width, width, 128)
        down_w[rows, :] = dot_l(act[:, rows], down_back[...]).astype(bf16)
        for i in range(CHIPS // DOWN_STEPS):
            chip = chunk * (CHIPS // DOWN_STEPS) + i
            for half in range(2):
                at = (chip * 2 + half) * (2 * PAIR_ROWS)
                pairs = [
                    (down_w.at[aligned(at + k * PAIR_ROWS, PAIR_ROWS, 16)], pl.ds(OUT_HALF + INNER_HALF + k * D, D))
                    for k in range(2)
                ]
                hand_over(place, chip, half, keep, send, pairs, wsem)

    def give(weights, half, width, lane):
        for chip in range(CHIPS):
            block = weights.at[pl.ds(chip * PAIR_ROWS, PAIR_ROWS), pl.ds(half * width, width)]
            hand_over(place, chip, half, keep, send, [(block, pl.ds(lane, width))], wsem)

    @pl.when((step >= inner_at) & (step < out_at))
    def _():
        cols = aligned((step - inner_at) * D, D, 128)
        inner_w[:, cols] = dot_l(hid[...], inner_back[:, cols]).astype(bf16)
        for half in range(2):

            @pl.when(step == inner_at + 2 * half + 1)
            def _():
                give(inner_w, half, INNER_HALF, OUT_HALF)

    @pl.when(step == out_at)
    def _():
        out_w[...] = dot_l(att[...], branch[...]).astype(bf16)
        for half in range(2):
            give(out_w, half, OUT_HALF, 0)
        wait_whole(keep, wsem)
        wait_whole(send, wsem)


def feed_forward(place, x, attended, cotangent, vectors, inner_bias, pieces, meta):
    count = x.shape[0]
    blocks = count // BLOCK
    last = blocks - 1
    token = lambda: pl.BlockSpec((BLOCK, D), lambda s: (jnp.minimum(s, last), 0))
    whole = lambda *shape: pl.BlockSpec(shape, lambda s: (0,) * len(shape))
    return pl.pallas_call(
        functools.partial(ffn_kernel, meta, len(pieces), blocks),
        grid=(blocks + DOWN_STEPS + INNER_STEPS + 1,),
        in_specs=[SMEM, token(), token(), token(), whole(16, D), whole(1, FF)] + [ANY] * len(pieces),
        out_specs=[token(), token(), token(), whole(8, D), whole(1, FF), ANY, ANY],
        out_shape=[
            jax.ShapeDtypeStruct((count, D), f32),
            jax.ShapeDtypeStruct((count, D), f32),
            jax.ShapeDtypeStruct((count, D), bf16),
            jax.ShapeDtypeStruct((8, D), f32),
            jax.ShapeDtypeStruct((1, FF), f32),
            jax.ShapeDtypeStruct((CHIPS, PAIR_ROWS, FFN_BLOCK), bf16),
            jax.ShapeDtypeStruct((CHIPS, PAIR_ROWS, FFN_BLOCK), bf16),
        ],
        scratch_shapes=[
            pltpu.VMEM((D, D), bf16),
            pltpu.VMEM((D, FF), bf16),
            pltpu.VMEM((FF, D), bf16),
            pltpu.VMEM((count, FF), bf16),
            pltpu.VMEM((count, FF), bf16),
            pltpu.VMEM((count, D), bf16),
            pltpu.VMEM((count, D), bf16),
            pltpu.VMEM((count, D), bf16),
            pltpu.VMEM((count, D), bf16),
            pltpu.VMEM((BLOCK, FF), f32),
            pltpu.SemaphoreType.DMA((3,)),
            pltpu.SemaphoreType.DMA,
        ],
        compiler_params=pltpu.CompilerParams(vmem_limit_bytes=62 * MIB),
        cost_estimate=pl.CostEstimate(flops=60_000_000_000, bytes_accessed=40 * MIB, transcendentals=0),
        name="feed_forward",
    )(place, x, attended, cotangent, vectors, inner_bias, *pieces)


def attend_back_pair(seq, pair, to, lengths, qkv_ref, back_ref, stat_ref, grads):
    rows = qkv_ref.shape[0]
    chunk = 256
    low, high = lane_masks()
    at = pair * 128
    queries = qkv_ref[:, aligned(at, 128, 128)]
    keys = qkv_ref[:, aligned(D + at, 128, 128)]
    values = qkv_ref[:, aligned(2 * D + at, 128, 128)]
    upstream = back_ref[:, aligned(at, 128, 128)]
    key_at = lax.broadcasted_iota(jnp.int32, (rows, 1), 0)
    hidden_keys = jnp.where(key_at < lengths[seq], 0.0, MASKED_SCORE).astype(f32)
    query_back = [jnp.zeros((chunk, 128), f32) for _ in range(rows // chunk)]
    key_back = jnp.zeros((rows, 128), f32)
    value_back = jnp.zeros((rows, 128), f32)
    for i, mask in enumerate((low, high)):
        own_keys, own_values = keys * mask, values * mask
        own_queries, own_up = queries * mask, upstream * mask
        for c in range(rows // chunk):
            span = slice(c * chunk, (c + 1) * chunk)
            log_total = stat_ref[0, pl.ds(2 * pair + i, 1), span]
            scores = dot_t(own_keys, queries[span]) * (0.125 * LOG2E) + hidden_keys
            weight = jnp.exp2(scores - log_total)
            weight_back = dot_t(own_values, upstream[span])
            mean = jnp.sum(weight * weight_back, axis=0, keepdims=True)
            score_back = (weight * (weight_back - mean)).astype(bf16)
            value_back += dot(weight.astype(bf16), own_up[span])
            key_back += dot(score_back, own_queries[span])
            query_back[c] += dot_l(score_back, own_keys)
    for c in range(rows // chunk):
        grads[aligned(to + c * chunk, chunk, chunk), aligned(at, 128, 128)] = (query_back[c] * 0.125).astype(bf16)
    grads[aligned(to, rows, rows), aligned(D + at, 128, 128)] = (key_back * 0.125).astype(bf16)
    grads[aligned(to, rows, rows), aligned(2 * D + at, 128, 128)] = value_back.astype(bf16)


def attend_back_first_kernel(lengths, qkv_ref, back_ref, stat_ref, grads):
    attend_back_pair(0, pl.program_id(0), 0, lengths, qkv_ref, back_ref, stat_ref, grads)


def attend_back_first(lengths, qkv, back, stats):
    rows = stats.shape[2]
    whole = lambda *shape: pl.BlockSpec(shape, lambda s: (0,) * len(shape))
    return pl.pallas_call(
        attend_back_first_kernel,
        grid=(H // 2,),
        in_specs=[SMEM, whole(rows, 3 * D), whole(rows, D), whole(1, 16, rows)],
        out_specs=whole(rows, 3 * D),
        out_shape=jax.ShapeDtypeStruct((rows, 3 * D), bf16),
        compiler_params=pltpu.CompilerParams(vmem_limit_bytes=56 * MIB),
        cost_estimate=pl.CostEstimate(flops=14_000_000_000, bytes_accessed=9 * MIB, transcendentals=0),
        name="attend_back_first",
    )(lengths, qkv, back, stats)


def attend_back_kernel(seqs, place, lengths, x_ref, qkv_ref, back_ref, stat_ref, small_ref, db1_ref, first, *refs):
    (grads_out, keep, send, grads, lowered, packed, sem, wsem) = refs
    step = pl.program_id(0)
    pairs = H // 2
    rows = stat_ref.shape[2]
    steps = (seqs - 1) * pairs
    first_in = pltpu.make_async_copy(first, grads.at[pl.ds(0, rows)], sem)
    whole_copy = pltpu.make_async_copy(grads, grads_out, sem)

    @pl.when(step == 0)
    def _():
        first_in.start()
        lowered[...] = x_ref[...].astype(bf16)

    @pl.when(step < steps)
    def _():
        seq = 1 + step // pairs
        attend_back_pair(seq, step % pairs, seq * rows, lengths, qkv_ref, back_ref, stat_ref, grads)

    @pl.when(step == steps)
    def _():
        first_in.wait()
        whole_copy.start()

    for which in range(3):

        @pl.when(step == steps + which)
        def _():
            g = dot_l(lowered[...], grads[:, which * D : (which + 1) * D]).astype(bf16)
            if which == 1:
                packed[:, D:QKV_HALF] = g[:, : D // 2]
                packed[:, QKV_BLOCK : QKV_BLOCK + D // 2] = g[:, D // 2 :]
            else:
                at = 0 if which == 0 else QKV_BLOCK + D // 2
                packed[:, at : at + D] = g

    @pl.when(step == steps + 2)
    def _():
        query_bias = jnp.sum(grads[:, 0:D].astype(f32), axis=0, keepdims=True)
        value_bias = jnp.sum(grads[:, 2 * D :].astype(f32), axis=0, keepdims=True)
        rows_of = jnp.concatenate([query_bias, value_bias, small_ref[2:8, :], jnp.zeros((120, D), f32)], axis=0)
        packed[:, QKV_HALF:QKV_BLOCK] = rows_of.T.astype(bf16)
        owner = lax.broadcasted_iota(jnp.int32, (SLABS, FF), 1) // (4 * SLAB)
        mine = jnp.where(owner == lax.broadcasted_iota(jnp.int32, (SLABS, FF), 0), db1_ref[...], 0.0)
        place_of = lax.broadcasted_iota(jnp.int32, (FF, 128), 0) % (4 * SLAB)
        pick = (place_of == lax.broadcasted_iota(jnp.int32, (FF, 128), 1)).astype(f32)
        table = lax.dot_general(
            mine, pick, (((1,), (0,)), ((), ())), precision=lax.Precision.HIGHEST, preferred_element_type=f32
        )
        spread = jnp.broadcast_to(table[:, None, :], (SLABS, SLAB, 128)).reshape(D, 128)
        packed[:, QKV_BLOCK + QKV_HALF :] = spread.astype(bf16)
        for chip in range(CHIPS):
            for half in range(2):
                block = packed.at[pl.ds(chip * PAIR_ROWS, PAIR_ROWS), pl.ds(half * QKV_BLOCK, QKV_BLOCK)]
                hand_over(place, chip, half, keep, send, [(block, pl.ds(0, QKV_BLOCK))], wsem)
        wait_whole(keep, wsem)
        wait_whole(send, wsem)
        whole_copy.wait()


def attend_back(place, lengths, x, qkv, back, stats, small, inner_bias_grad, first):
    seqs = lengths.shape[0]
    count = x.shape[0]
    rows = count // seqs
    pairs = H // 2
    seq_of = lambda s: jnp.minimum(1 + s // pairs, seqs - 1)
    whole = lambda *shape: pl.BlockSpec(shape, lambda s: (0,) * len(shape))
    return pl.pallas_call(
        functools.partial(attend_back_kernel, seqs),
        grid=((seqs - 1) * pairs + 3,),
        in_specs=[
            SMEM,
            SMEM,
            whole(count, D),
            pl.BlockSpec((rows, 3 * D), lambda s: (seq_of(s), 0)),
            pl.BlockSpec((rows, D), lambda s: (seq_of(s), 0)),
            pl.BlockSpec((1, 16, rows), lambda s: (seq_of(s), 0, 0)),
            whole(8, D),
            whole(1, FF),
            ANY,
        ],
        out_specs=[ANY, ANY, ANY],
        out_shape=[
            jax.ShapeDtypeStruct((count, 3 * D), bf16),
            jax.ShapeDtypeStruct((CHIPS, PAIR_ROWS, QKV_BLOCK), bf16),
            jax.ShapeDtypeStruct((CHIPS, PAIR_ROWS, QKV_BLOCK), bf16),
        ],
        scratch_shapes=[
            pltpu.VMEM((count, 3 * D), bf16),
            pltpu.VMEM((count, D), bf16),
            pltpu.VMEM((D, 2 * QKV_BLOCK), bf16),
            pltpu.SemaphoreType.DMA,
            pltpu.SemaphoreType.DMA,
        ],
        compiler_params=pltpu.CompilerParams(vmem_limit_bytes=56 * MIB),
        cost_estimate=pl.CostEstimate(flops=23_000_000_000, bytes_accessed=20 * MIB, transcendentals=0),
        name="attend_back",
    )(place, lengths, x, qkv, back, stats, small, inner_bias_grad, first)


def input_back_kernel(fb_ref, grads_ref, w_ref, out_ref):
    half = D + D // 2
    first = dot_t(grads_ref[:, 0:half], w_ref[:, 0:half])
    second = dot_t(grads_ref[:, half:], w_ref[:, QKV_BLOCK : QKV_BLOCK + half])
    out_ref[...] = fb_ref[...] + first + second


def input_back(first_back, grads, weights):
    count = first_back.shape[0]
    return pl.pallas_call(
        input_back_kernel,
        grid=(count // BLOCK,),
        in_specs=[
            pl.BlockSpec((BLOCK, D), lambda s: (s, 0)),
            pl.BlockSpec((BLOCK, 3 * D), lambda s: (s, 0)),
            pl.BlockSpec((D, 2 * QKV_BLOCK), lambda s: (0, 0)),
        ],
        out_specs=pl.BlockSpec((BLOCK, D), lambda s: (s, 0)),
        out_shape=jax.ShapeDtypeStruct((count, D), f32),
        compiler_params=pltpu.CompilerParams(vmem_limit_bytes=56 * MIB),
        cost_estimate=pl.CostEstimate(flops=9_000_000_000, bytes_accessed=15 * MIB, transcendentals=0),
        name="input_back",
    )(first_back, grads, weights)


AXES = ("dp", "fsdp")


def swap(v, mask, count):
    return lax.ppermute(v, AXES, [(i, i ^ mask) for i in range(count)])


CORE, ALONG_X, ALONG_Y, ALONG_Z = 1, 2, 4, 8
Z_COUNT = 4
FAST_SHAPE = {"dp": Z_COUNT, "fsdp": 8}


def after(values, *others):
    out = lax.optimization_barrier(tuple(values) + others)
    return out[: len(values)]


def move(v, mask):
    return swap(v, mask, SLABS)


def gather_z(block):
    return [block] + [move(block, k * ALONG_Z) for k in range(1, Z_COUNT)]


def gather_one(per_z):
    first, second = jnp.stack(per_z[:2]), jnp.stack(per_z[2:])
    return first, second, move(first, ALONG_X), move(second, ALONG_Y)


def gather_two(state):
    first, second, first_x, second_y = state
    first_chips, second_chips = (0, 4), (8, 12)
    shift = lambda chips, by: tuple(c ^ by for c in chips)
    first = jnp.concatenate([first, first_x])
    second = jnp.concatenate([second, second_y])
    first_chips += shift(first_chips, 1)
    second_chips += shift(second_chips, 2)
    return [
        (first, first_chips),
        (second, second_chips),
        (move(first, ALONG_Y), shift(first_chips, 2)),
        (move(second, ALONG_X), shift(second_chips, 1)),
    ]


def gather_core(held):
    arrays = [a for a, _ in held] + [move(a, CORE) for a, _ in held]
    meta = tuple((c, False) for _, c in held) + tuple((c, True) for _, c in held)
    return arrays, meta


def wide(v):
    return v.astype(f32)


LOW_Z, HIGH_Z, EVERY = slice(0, 2), slice(2, 4), slice(None)


class ChipSums:
    def __init__(self, keep, got):
        shape = (Z_COUNT, 2, 2) + keep.shape[1:]
        self.keep, self.got = keep.reshape(shape), got.reshape(shape)

    def part(self, z, y, x):
        return wide(self.keep[z, y, x]) + wide(self.got[z, y, x])


def scatter_ready(sums):
    return sums.part(LOW_Z, 1, EVERY).astype(bf16), sums.part(HIGH_Z, EVERY, 1).astype(bf16)


def scatter_one(first, second):
    return move(first, ALONG_Y), move(second, ALONG_X)


def scatter_two(sums, first, second):
    first_sum = lambda x: sums.part(LOW_Z, 0, x) + wide(first[:, x])
    second_sum = lambda y: sums.part(HIGH_Z, y, 0) + wide(second[:, y])
    first_more = move(first_sum(1).astype(bf16), ALONG_X)
    second_more = move(second_sum(1).astype(bf16), ALONG_Y)
    low_part = first_sum(0) + wide(first_more)
    high_part = second_sum(0) + wide(second_more)
    return [low_part[0], low_part[1], high_part[0], high_part[1]]


def scatter_z(parts):
    total = parts[0]
    for k in range(1, Z_COUNT):
        total = total + wide(move(parts[k].astype(bf16), k * ALONG_Z))
    return total


def fast_blocks(shards, core):
    (qw, kw, vw, ow, qb, vb, ob, fg, fs, iw, ib, dw, db, sg, ss) = shards
    vectors = jnp.pad(jnp.stack([qb, vb, ob, fg, fs, db, sg, ss], axis=1), ((0, 0), (0, 120)))
    inner_bias = jnp.pad(ib.reshape(1, 4 * SLAB), ((0, SLAB - 1), (0, 128 - 4 * SLAB)))
    half = D // 2
    halves = [
        jnp.concatenate([qw, kw[:, :half], vectors, ow[:, :half], iw[:, :INNER_HALF]], axis=1),
        jnp.concatenate([kw[:, half:], vw, inner_bias, ow[:, half:], iw[:, INNER_HALF:]], axis=1),
    ]
    low_core = core == 0
    own = jnp.where(low_core, halves[0], halves[1])
    other = move(jnp.where(low_core, halves[1], halves[0]), CORE)
    rows = jnp.concatenate([jnp.where(low_core, own, other), jnp.where(low_core, other, own)], axis=0)
    qkv_block = rows[:, :QKV_BLOCK]
    ffn_block = jnp.concatenate([rows[:, QKV_BLOCK:], dw[:PAIR_ROWS], dw[PAIR_ROWS:]], axis=1)
    return qkv_block, ffn_block


def both_halves(total, core):
    mine = lax.dynamic_slice_in_dim(total, core * SLAB, SLAB, 0)
    other = move(lax.dynamic_slice_in_dim(total, (1 - core) * SLAB, SLAB, 0), CORE)
    low_core = core == 0
    return jnp.where(low_core, mine, other), jnp.where(low_core, other, mine)


def gather_plain(shards):
    (qw, kw, vw, ow, qb, vb, ob, fg, fs, iw, ib, dw, db, sg, ss) = [
        lax.all_gather(v, AXES, axis=0, tiled=True) for v in shards
    ]
    vectors = jnp.pad(jnp.stack([qb, vb, ob, fg, fs, db, sg, ss], axis=1), ((0, 0), (0, 120)))
    inner_bias = jnp.pad(ib.reshape(SLABS, 1, 4 * SLAB), ((0, 0), (0, SLAB - 1), (0, 128 - 4 * SLAB))).reshape(D, 128)
    half = D // 2
    chips = lambda v: v.reshape(CHIPS, PAIR_ROWS, -1)
    down = dw.reshape(CHIPS, 2, 2, PAIR_ROWS, D)
    first = [
        chips(jnp.concatenate([qw, kw[:, :half], vectors], axis=1)),
        chips(jnp.concatenate([kw[:, half:], vw, inner_bias], axis=1)),
    ]
    second = [
        jnp.concatenate(
            [
                chips(ow[:, c * half : (c + 1) * half]),
                chips(iw[:, c * INNER_HALF : (c + 1) * INNER_HALF]),
                down[:, c, 0],
                down[:, c, 1],
            ],
            axis=2,
        )
        for c in range(2)
    ]
    meta = ((tuple(range(CHIPS)), False), (tuple(range(CHIPS)), True))
    return (first, meta), (second, meta)


def local(fast, inputs, lengths, *rest):
    shards, cotangent = rest[:15], rest[15]
    if fast:
        linear = lax.axis_index(AXES)
        core = linear & 1
        place = jnp.stack([linear >> 1, core]).astype(jnp.int32)
        qkv_block, ffn_block = fast_blocks(shards, core)
        qkv_z = gather_z(qkv_block)
        (ffn_block,) = after((ffn_block,), *qkv_z[1:])
        ffn_z = gather_z(ffn_block)
        qkv_two = gather_two(gather_one(qkv_z))
        first, first_meta = gather_core(qkv_two)
        ffn_z = after(ffn_z, *(v for v, _ in qkv_two))
        ffn_one = gather_one(ffn_z)
    else:
        place = jnp.zeros((2,), jnp.int32)
        (first, first_meta), (second, second_meta) = gather_plain(shards)
    qkv, attended, stats, weights, vectors = attend(place, lengths, inputs, first, first_meta)
    bias_at = QKV_BLOCK + QKV_HALF
    inner_bias = weights[::SLAB, bias_at : bias_at + 4 * SLAB].reshape(1, FF).astype(f32)
    if fast:
        ffn_one = after(ffn_one, attended)
        second, second_meta = gather_core(gather_two(ffn_one))
    output, first_back, back, small, db1, ffn_keep, ffn_send = feed_forward(
        place, inputs, attended, cotangent, vectors, inner_bias, second, second_meta
    )
    half_grads = attend_back_first(lengths, qkv, back, stats)
    if fast:
        ffn_got = move(ffn_send, CORE)
        (ffn_got,) = after((ffn_got,), half_grads)
        ffn_sums = ChipSums(ffn_keep, ffn_got)
        ffn_ready = scatter_ready(ffn_sums)
        half_grads, *ffn_ready = after((half_grads,) + ffn_ready)
        ffn_first = scatter_one(*ffn_ready)
    grads, qkv_keep, qkv_send = attend_back(place, lengths, inputs, qkv, back, stats, small, db1, half_grads)
    if fast:
        qkv_got = move(qkv_send, CORE)
        ffn_first = after(ffn_first, qkv_keep)
        ffn_parts = scatter_two(ffn_sums, *ffn_first)
        qkv_sums = ChipSums(qkv_keep, qkv_got)
        ffn = scatter_z(ffn_parts)
        proj = scatter_z(scatter_two(qkv_sums, *scatter_one(*scatter_ready(qkv_sums))))
        grad_input = input_back(first_back, grads, weights)
        narrow = both_halves(ffn[:, : OUT_HALF + INNER_HALF], core)
        down_grad = jnp.concatenate([ffn[:, -2 * D : -D], ffn[:, -D:]], axis=0)
        proj = both_halves(proj, core)
        shard = lambda v: v
    else:
        grad_input = input_back(first_back, grads, weights)
        shard = lambda v: lax.psum_scatter(v, AXES, scatter_dimension=0, tiled=True)
        flat = lambda v: v.astype(f32).reshape(D, -1)
        narrow = [flat(v[:, :, : OUT_HALF + INNER_HALF]) for v in (ffn_keep, ffn_send)]
        parts = [jnp.stack([v[:, :, -2 * D : -D], v[:, :, -D:]], axis=1) for v in (ffn_keep, ffn_send)]
        down_grad = jnp.stack(parts, axis=1).reshape(FF, D).astype(f32)
        proj = [flat(v) for v in (qkv_keep, qkv_send)]
    low, high = proj
    wide = lambda *v: shard(jnp.concatenate(v, axis=1))
    vec = lambda i: shard(low[:, QKV_HALF + i])
    return (
        output,
        grad_input,
        shard(low[:, :D]),
        wide(low[:, D:QKV_HALF], high[:, : D // 2]),
        shard(high[:, D // 2 : QKV_HALF]),
        wide(narrow[0][:, :OUT_HALF], narrow[1][:, :OUT_HALF]),
        vec(0),
        vec(1),
        vec(2),
        vec(3),
        vec(4),
        wide(narrow[0][:, OUT_HALF:], narrow[1][:, OUT_HALF:]),
        shard(high[::SLAB, QKV_HALF : QKV_HALF + 4 * SLAB].reshape(-1)),
        shard(down_grad),
        vec(5),
        vec(6),
        vec(7),
    )


def solution(mesh):
    rows, flat = P(AXES, None), P(AXES)
    params = (rows,) * 4 + (flat,) * 5 + (rows, flat, rows, flat, flat, flat)
    return jax.shard_map(
        functools.partial(local, dict(mesh.shape) == FAST_SHAPE),
        mesh=mesh,
        in_specs=(rows, flat) + params + (rows,),
        out_specs=(rows, rows) + params,
        check_vma=False,
    )
```

time: 376 us -> 307 us (0.82)
  waiting for transfers between devices: 160 us -> 106 us
  Pallas kernels: 142 us -> 127 us
    ppermute x39 -> x41, waiting for transfers between devices: 160 us -> 106 us  [swap(): return lax.ppermute(v, AXES, [(i, i ^ mask) for i in range(count)])]
    pallas_call x1, Pallas kernels: 74.7 us -> 60.2 us  [feed_forward(): pl.pallas_call(functools.partial(ffn_kernel, meta, len(pieces), blocks),...]
    ppermute x39 -> x41, starting transfers between devices: 41.6 us -> 44.9 us  [swap(): return lax.ppermute(v, AXES, [(i, i ^ mask) for i in range(count)])]
    pallas_call x1 -> x2, Pallas kernels: 40.6 us -> 40.2 us  [the longest x1 24 us: attend_back(): pl.pallas_call(functools.partial(attend_back_kernel, seqs), grid=((seqs -...]
  transfers between devices with their start and end apart: 39 -> 41, of which waited for: 18 -> 18; matrix products, arithmetic and copies ran while one was open for 5% -> 4% of each run, Pallas kernels for 18% -> 22%
where the time goes in v2:
time: 307 us
  Pallas kernels  127 us (41%)
  waiting for transfers between devices  106 us (35%)
  starting transfers between devices  44.9 us (15%)
  other arithmetic  16 us (5%)
  local copies, waits for them, and re-layouts  11.9 us (4%)
    ppermute x41, waiting for transfers between devices, swap(): return lax.ppermute(v, AXES, [(i, i ^ mask) for i in range(count)])  106 us
    pallas_call x1, Pallas kernels, feed_forward(): pl.pallas_call(functools.partial(ffn_kernel, meta, len(pieces), blocks),...  60.2 us
    ppermute x41, starting transfers between devices, swap(): return lax.ppermute(v, AXES, [(i, i ^ mask) for i in range(count)])  44.9 us
    pallas_call x1, Pallas kernels, attend_back(): pl.pallas_call(functools.partial(attend_back_kernel, seqs), grid=((seqs -...  24 us
    pallas_call x1, Pallas kernels, attend(): pl.pallas_call(functools.partial(attend_kernel, meta, len(pieces)), grid=...  17 us
    pallas_call x1, Pallas kernels, attend_back_first(): pl.pallas_call(attend_back_first_kernel, grid=(H // 2,), in_specs=[SMEM,...  16.2 us
    pallas_call x1, Pallas kernels, input_back(): pl.pallas_call(input_back_kernel, grid=(count // BLOCK,), in_specs=[pl.Bl...  9.39 us
  transfers between devices with their start and end apart: 41, of which 18 were waited for; matrix products, arithmetic and copies ran while one was open for 4% of the time, Pallas kernels for 22%

profile of v2, /device:TPU:0, one launch (start us, length us, event | category | flops | bytes accessed | tf_op | source)
XLA Modules:
  0.0 306.6 jit_solution(14624374287814218385)
XLA Ops:
  7.8 3.0 collective-permute-start.1
  10.8 2.5 collective-permute-start.4
  14.5 1.7 collective-permute-start.2
  16.2 4.0 %collective-permute-done.4 = bf16[48,1280]{1,0:T(8,128)(2,1)S(1)} collective-permute-done((bf16[48,1280]{1,0:T(8,128)(2,1)S(1)}, bf16[48,1280]{1,0:T(8,128)(2,1)S(1)}, u32[]{:S(2)}, u32[]{:S(2)}) %collective-permute-start.4) | collective-permute-done | bytes 122912 | tf_op jit(solution)/shard_map/ppermute | solution.py:563
  20.2 4.5 %collective-permute-done.3 = bf16[48,1280]{1,0:T(8,128)(2,1)S(1)} collective-permute-done((bf16[48,1280]{1,0:T(8,128)(2,1)S(1)}, bf16[48,1280]{1,0:T(8,128)(2,1)S(1)}, u32[]{:S(2)}, u32[]{:S(2)}) %collective-permute-start.3) | collective-permute-done | bytes 122912 | tf_op jit(solution)/shard_map/ppermute | solution.py:563
  26.9 6.7 %collective-permute-done.5 = bf16[2,48,1280]{2,1,0:T(8,128)(2,1)S(1)} collective-permute-done((bf16[2,48,1280]{2,1,0:T(8,128)(2,1)S(1)}, bf16[2,48,1280]{2,1,0:T(8,128)(2,1)S(1)}, u32[]{:S(2)}, u32[]{:S(2)}) %collective-permute-start.5) | collective-permute-done | bytes 245792 | tf_op jit(solution)/shard_map/ppermute | solution.py:563
  35.4 3.2 %collective-permute-start.13 = (bf16[48,3456]{1,0:T(8,128)(2,1)S(1)}, bf16[48,3456]{1,0:T(8,128)(2,1)S(1)}, u32[]{:S(2)}, u32[]{:S(2)}) collective-permute-start(bf16[48,3456]{1,0:T(8,128)(2,1)S(1)} %fusion.19), channel_id=1, source_target_pairs={{0,16},{1,17},{2,18},{3,19},{4,20},{5,21},{6,22},{7,23},{8,24},{9,... | collective-permute-start | bytes 995336 | tf_op jit(solution)/shard_map/ppermute | solution.py:563
  40.3 9.3 %collective-permute-done.12 = bf16[48,3456]{1,0:T(8,128)(2,1)S(1)} collective-permute-done((bf16[48,3456]{1,0:T(8,128)(2,1)S(1)}, bf16[48,3456]{1,0:T(8,128)(2,1)S(1)}, u32[]{:S(2)}, u32[]{:S(2)}) %collective-permute-start.12) | collective-permute-done | bytes 331808 | tf_op jit(solution)/shard_map/ppermute | solution.py:563
  49.6 10.5 %collective-permute-done.13 = bf16[48,3456]{1,0:T(8,128)(2,1)S(1)} collective-permute-done((bf16[48,3456]{1,0:T(8,128)(2,1)S(1)}, bf16[48,3456]{1,0:T(8,128)(2,1)S(1)}, u32[]{:S(2)}, u32[]{:S(2)}) %collective-permute-start.13) | collective-permute-done | bytes 331808 | tf_op jit(solution)/shard_map/ppermute | solution.py:563
  64.9 17.0 %attend.1 = (bf16[1024,2304]{1,0:T(8,128)(2,1)}, bf16[1024,768]{1,0:T(8,128)(2,1)}, f32[2,16,512]{2,1,0:T(8,128)}, bf16[768,2560]{1,0:T(8,128)(2,1)}, f32[16,768]{1,0:T(8,128)}) custom-call(s32[2]{0:T(128)} %pad_add_fusion.place, s32[2]{0:T(128)} %lengths.5, f32[1024,768]{1,0:T(8,128)} %x_ref.5, bf16[4,48,1280]{2,1,0:T(8,128)(2,1)} %copy-done.2, ...), custom_call_target="tpu_custom_call" | custom-call | flops 17999998976 | bytes 20971520 | tf_op jit(solution)/shard_map/attend/pallas_call | solution.py:169
  84.9 28.4 %collective-permute-done.17.refs_2_ = bf16[4,48,3456]{2,1,0:T(8,128)(2,1)} collective-permute-done((bf16[4,48,3456]{2,1,0:T(8,128)(2,1)S(1)}, bf16[4,48,3456]{2,1,0:T(8,128)(2,1)}, u32[]{:S(2)}, u32[]{:S(2)}) %collective-permute-start.17) | collective-permute-done | bytes 1327136 | tf_op jit(solution)/shard_map/ppermute | solution.py:563
  116.7 1.9 collective-permute-done.22.refs_7_
  118.6 60.2 %feed_forward.1 = (f32[1024,768]{1,0:T(8,128)}, f32[1024,768]{1,0:T(8,128)}, bf16[1024,768]{1,0:T(8,128)(2,1)}, f32[8,768]{1,0:T(8,128)}, f32[1,3072]{1,0:T(1,12...) custom-call(s32[2]{0:T(128)} %pad_add_fusion.place, f32[1024,768]{1,0:T(8,128)} %x_ref.5, ...), custom_call_target="tpu_custom_call" | custom-call | flops 60000002048 | bytes 41943040 | tf_op jit(solution)/shard_map/feed_forward/pallas_call | solution.py:347
  179.0 16.2 %attend_back_first.1.first = bf16[512,2304]{1,0:T(8,128)(2,1)} custom-call(s32[2]{0:T(128)} %lengths.5, bf16[1024,2304]{1,0:T(8,128)(2,1)} %get-tuple-element.61.qkv_ref, bf16[1024,768]{1,0:T(8,128)(2,1)} %get-tuple-element.62.back_ref, f32[2,16,512]{2,1,0:T(8,128)} %get-tuple-element.63.stat_ref), custom_call_target="tpu_custom_call" | custom-call | flops 14000000000 | bytes 9437184 | tf_op jit(solution)/shard_map/attend_back_first/pallas_call | solution.py:422
  195.2 2.7 fusion
  197.9 2.7 fusion.1
  202.6 24.0 %attend_back.1 = (bf16[1024,2304]{1,0:T(8,128)(2,1)}, bf16[16,48,1280]{2,1,0:T(8,128)(2,1)}, bf16[16,48,1280]{2,1,0:T(8,128)(2,1)}) custom-call(s32[2]{0:T(128)} %pad_add_fusion.place, s32[2]{0:T(128)} %lengths.5, f32[1024,768]{1,0:T(8,128)} %x_ref.5, bf16[1024,2304]{1,0:T(8,128)(2,1)} %get-tuple-element.61.qkv_ref, ...), custom_call_target="tpu_custom_call" | custom-call | flops 23000000512 | bytes 20971520 | tf_op jit(solution)/shard_map/attend_back/pallas_call | solution.py:501
  226.6 9.4 %input_back.1 = f32[1024,768]{1,0:T(8,128)} custom-call(f32[1024,768]{1,0:T(8,128)} %get-tuple-element.60.fb_ref, bf16[1024,2304]{1,0:T(8,128)(2,1)} %get-tuple-element.70.grads_ref, bf16[768,2560]{1,0:T(8,128)(2,1)} %get-tuple-element.49.w_ref), custom_call_target="tpu_custom_call" | custom-call | flops 8999999488 | bytes 15728640 | tf_op jit(solution)/shard_map/input_back/pallas_call | solution.py:543
  236.0 1.7 fusion.2
  237.7 1.6 collective-permute-start.37
  241.3 14.1 %collective-permute-done.37 = bf16[2,48,3456]{2,1,0:T(8,128)(2,1)S(1)} collective-permute-done((bf16[2,48,3456]{2,1,0:T(8,128)(2,1)S(1)}, bf16[2,48,3456]{2,1,0:T(8,128)(2,1)S(1)}, u32[]{:S(2)}, u32[]{:S(2)}) %collective-permute-start.37) | collective-permute-done | bytes 663584 | tf_op jit(solution)/shard_map/ppermute | solution.py:563
  255.5 2.5 fusion.4
  259.2 2.5 collective-permute-start.39
  261.7 3.0 collective-permute-start.38
  266.0 8.1 %collective-permute-done.35 = bf16[2,48,3456]{2,1,0:T(8,128)(2,1)S(1)} collective-permute-done((bf16[2,48,3456]{2,1,0:T(8,128)(2,1)S(1)}, bf16[2,48,3456]{2,1,0:T(8,128)(2,1)S(1)}, u32[]{:S(2)}, u32[]{:S(2)}) %collective-permute-start.35) | collective-permute-done | bytes 663584 | tf_op jit(solution)/shard_map/ppermute | solution.py:563
  274.1 1.8 fusion.6
  275.9 4.3 %collective-permute-start.36 = (bf16[48,3456]{1,0:T(8,128)(2,1)S(1)}, bf16[48,3456]{1,0:T(8,128)(2,1)S(1)}, u32[]{:S(2)}, u32[]{:S(2)}) collective-permute-start(bf16[48,3456]{1,0:T(8,128)(2,1)S(1)} %fusion.17), channel_id=1, source_target_pairs={{0,8},{1,9},{2,10},{3,11},{4,12},{5,13},{6,14},{7,15},{8,0},{9,1},... | collective-permute-start | bytes 995336 | tf_op jit(solution)/shard_map/ppermute | solution.py:563
  281.5 1.9 collective-permute-start.31
  283.4 3.3 %collective-permute-done.26 = bf16[2,48,1280]{2,1,0:T(8,128)(2,1)S(1)} collective-permute-done((bf16[2,48,1280]{2,1,0:T(8,128)(2,1)S(1)}, bf16[2,48,1280]{2,1,0:T(8,128)(2,1)S(1)}, u32[]{:S(2)}, u32[]{:S(2)}) %collective-permute-start.26) | collective-permute-done | bytes 245792 | tf_op jit(solution)/shard_map/ppermute | solution.py:563
  287.3 2.1 collective-permute-start.27
  289.3 7.2 %collective-permute-done.38 = bf16[48,3456]{1,0:T(8,128)(2,1)S(1)} collective-permute-done((bf16[48,3456]{1,0:T(8,128)(2,1)S(1)}, bf16[48,3456]{1,0:T(8,128)(2,1)S(1)}, u32[]{:S(2)}, u32[]{:S(2)}) %collective-permute-start.38) | collective-permute-done | bytes 331808 | tf_op jit(solution)/shard_map/ppermute | solution.py:563
  298.7 3.0 collective-permute-done.30
  (143 shorter events, 40.7 us)
Async XLA Ops:
  7.8 6.6 %collective-permute-start.1 = (bf16[48,1280]{1,0:T(8,128)(2,1)S(1)}, bf16[48,1280]{1,0:T(8,128)(2,1)S(1)}, u32[]{:S(2)}, u32[]{:S(2)}) collective-permute-start(bf16[48,1280]{1,0:T(8,128)(2,1)S(1)} %pad_maximum_fusion.9), channel_id=1, source_target_pairs={{0,8},{1,9},{2,10},{3,11},{4,12},{5,13},{6,14},{7,15},{8,0},{9,1},... | collective-permute-start | bytes 368648 | tf_op jit(solution)/shard_map/ppermute | solution.py:563
  10.8 9.3 %collective-permute-start.4 = (bf16[48,1280]{1,0:T(8,128)(2,1)S(1)}, bf16[48,1280]{1,0:T(8,128)(2,1)S(1)}, u32[]{:S(2)}, u32[]{:S(2)}) collective-permute-start(bf16[48,1280]{1,0:T(8,128)(2,1)S(1)} %pad_maximum_fusion.9), channel_id=1, source_target_pairs={{0,24},{1,25},{2,26},{3,27},{4,28},{5,29},{6,30},{7,31},{8,16},{9,... | collective-permute-start | bytes 368648 | tf_op jit(solution)/shard_map/ppermute | solution.py:563
  13.3 11.4 %collective-permute-start.3 = (bf16[48,1280]{1,0:T(8,128)(2,1)S(1)}, bf16[48,1280]{1,0:T(8,128)(2,1)S(1)}, u32[]{:S(2)}, u32[]{:S(2)}) collective-permute-start(bf16[48,1280]{1,0:T(8,128)(2,1)S(1)} %pad_maximum_fusion.9), channel_id=1, source_target_pairs={{0,16},{1,17},{2,18},{3,19},{4,20},{5,21},{6,22},{7,23},{8,24},{9,... | collective-permute-start | bytes 368648 | tf_op jit(solution)/shard_map/ppermute | solution.py:563
  14.5 11.8 %collective-permute-start.2 = (bf16[2,48,1280]{2,1,0:T(8,128)(2,1)S(1)}, bf16[2,48,1280]{2,1,0:T(8,128)(2,1)S(1)}, u32[]{:S(2)}, u32[]{:S(2)}) collective-permute-start(bf16[2,48,1280]{2,1,0:T(8,128)(2,1)S(1)} %pad_maximum_fusion.7), channel_id=1, source_target_pairs={{0,2},{1,3},{2,0},{3,1},{4,6},{5,7},{6,4},{7,5},{8,10},{9,11},{10,... | collective-permute-start | bytes 737288 | tf_op jit(solution)/shard_map/ppermute | solution.py:563
  24.7 9.0 %collective-permute-start.5 = (bf16[2,48,1280]{2,1,0:T(8,128)(2,1)S(1)}, bf16[2,48,1280]{2,1,0:T(8,128)(2,1)S(1)}, u32[]{:S(2)}, u32[]{:S(2)}) collective-permute-start(bf16[2,48,1280]{2,1,0:T(8,128)(2,1)S(1)} %pad_maximum_fusion.8), channel_id=1, source_target_pairs={{0,4},{1,5},{2,6},{3,7},{4,0},{5,1},{6,2},{7,3},{8,12},{9,13},{10,... | collective-permute-start | bytes 737288 | tf_op jit(solution)/shard_map/ppermute | solution.py:563
  26.4 33.8 %collective-permute-start.6 = (bf16[4,48,1280]{2,1,0:T(8,128)(2,1)S(1)}, bf16[4,48,1280]{2,1,0:T(8,128)(2,1)S(1)}, u32[]{:S(2)}, u32[]{:S(2)}) collective-permute-start(bf16[4,48,1280]{2,1,0:T(8,128)(2,1)S(1)} %pad_maximum_fusion.2.refs_0_), channel_id=1, source_target_pairs={{0,4},{1,5},{2,6},{3,7},{4,0},{5,1},{6,2},{7,3},{8,12},{9,13},{10,... | collective-permute-start | bytes 1474568 | tf_op jit(solution)/shard_map/ppermute | solution.py:563
  33.7 26.5 %collective-permute-start.7 = (bf16[4,48,1280]{2,1,0:T(8,128)(2,1)S(1)}, bf16[4,48,1280]{2,1,0:T(8,128)(2,1)S(1)}, u32[]{:S(2)}, u32[]{:S(2)}) collective-permute-start(bf16[4,48,1280]{2,1,0:T(8,128)(2,1)S(1)} %pad_maximum_fusion.3.refs_1_), channel_id=1, source_target_pairs={{0,2},{1,3},{2,0},{3,1},{4,6},{5,7},{6,4},{7,5},{8,10},{9,11},{10,... | collective-permute-start | bytes 1474568 | tf_op jit(solution)/shard_map/ppermute | solution.py:563
  35.3 14.3 %collective-permute-start.12 = (bf16[48,3456]{1,0:T(8,128)(2,1)S(1)}, bf16[48,3456]{1,0:T(8,128)(2,1)S(1)}, u32[]{:S(2)}, u32[]{:S(2)}) collective-permute-start(bf16[48,3456]{1,0:T(8,128)(2,1)S(1)} %fusion.19), channel_id=1, source_target_pairs={{0,8},{1,9},{2,10},{3,11},{4,12},{5,13},{6,14},{7,15},{8,0},{9,1},... | collective-permute-start | bytes 995336 | tf_op jit(solution)/shard_map/ppermute | solution.py:563
  35.4 24.8 %collective-permute-start.13 = (bf16[48,3456]{1,0:T(8,128)(2,1)S(1)}, bf16[48,3456]{1,0:T(8,128)(2,1)S(1)}, u32[]{:S(2)}, u32[]{:S(2)}) collective-permute-start(bf16[48,3456]{1,0:T(8,128)(2,1)S(1)} %fusion.19), channel_id=1, source_target_pairs={{0,16},{1,17},{2,18},{3,19},{4,20},{5,21},{6,22},{7,23},{8,24},{9,... | collective-permute-start | bytes 995336 | tf_op jit(solution)/shard_map/ppermute | solution.py:563
  38.6 21.6 %collective-permute-start.14 = (bf16[48,3456]{1,0:T(8,128)(2,1)S(1)}, bf16[48,3456]{1,0:T(8,128)(2,1)S(1)}, u32[]{:S(2)}, u32[]{:S(2)}) collective-permute-start(bf16[48,3456]{1,0:T(8,128)(2,1)S(1)} %fusion.19), channel_id=1, source_target_pairs={{0,24},{1,25},{2,26},{3,27},{4,28},{5,29},{6,30},{7,31},{8,16},{9,... | collective-permute-start | bytes 995336 | tf_op jit(solution)/shard_map/ppermute | solution.py:563
  49.6 12.0 %collective-permute-start.8 = (bf16[4,48,1280]{2,1,0:T(8,128)(2,1)S(1)}, bf16[4,48,1280]{2,1,0:T(8,128)(2,1)S(1)}, u32[]{:S(2)}, u32[]{:S(2)}) collective-permute-start(bf16[4,48,1280]{2,1,0:T(8,128)(2,1)S(1)} %pad_maximum_fusion.2.refs_0_), channel_id=1, source_target_pairs={{0,1},{1,0},{2,3},{3,2},{4,5},{5,4},{6,7},{7,6},{8,9},{9,8},{10,11... | collective-permute-start | bytes 1474568 | tf_op jit(solution)/shard_map/ppermute | solution.py:563
  60.9 21.1 %collective-permute-start.15 = (bf16[2,48,3456]{2,1,0:T(8,128)(2,1)S(1)}, bf16[2,48,3456]{2,1,0:T(8,128)(2,1)S(1)}, u32[]{:S(2)}, u32[]{:S(2)}) collective-permute-start(bf16[2,48,3456]{2,1,0:T(8,128)(2,1)S(1)} %pad_maximum_fusion), channel_id=1, source_target_pairs={{0,2},{1,3},{2,0},{3,1},{4,6},{5,7},{6,4},{7,5},{8,10},{9,11},{10,... | collective-permute-start | bytes 1990664 | tf_op jit(solution)/shard_map/ppermute | solution.py:563
  61.6 20.4 %collective-permute-start.16 = (bf16[2,48,3456]{2,1,0:T(8,128)(2,1)S(1)}, bf16[2,48,3456]{2,1,0:T(8,128)(2,1)S(1)}, u32[]{:S(2)}, u32[]{:S(2)}) collective-permute-start(bf16[2,48,3456]{2,1,0:T(8,128)(2,1)S(1)} %pad_maximum_fusion.1), channel_id=1, source_target_pairs={{0,4},{1,5},{2,6},{3,7},{4,0},{5,1},{6,2},{7,3},{8,12},{9,13},{10,... | collective-permute-start | bytes 1990664 | tf_op jit(solution)/shard_map/ppermute | solution.py:563
  82.2 31.1 %collective-permute-start.17 = (bf16[4,48,3456]{2,1,0:T(8,128)(2,1)S(1)}, bf16[4,48,3456]{2,1,0:T(8,128)(2,1)}, u32[]{:S(2)}, u32[]{:S(2)}) collective-permute-start(bf16[4,48,3456]{2,1,0:T(8,128)(2,1)S(1)} %constant_dynamic-update-slice_fusion.8.refs_0_), channel_id=1, source_target_pairs={{0,4},{1,5},{2,6},{3,7},{4,0},{5,1},{6,2},{7,3},{8,12},{9,13},{10,... | collective-permute-start | bytes 3981320 | tf_op jit(solution)/shard_map/ppermute | solution.py:563
  83.2 31.1 %collective-permute-start.18 = (bf16[4,48,3456]{2,1,0:T(8,128)(2,1)S(1)}, bf16[4,48,3456]{2,1,0:T(8,128)(2,1)}, u32[]{:S(2)}, u32[]{:S(2)}) collective-permute-start(bf16[4,48,3456]{2,1,0:T(8,128)(2,1)S(1)} %constant_dynamic-update-slice_fusion.10.refs_1_), channel_id=1, source_target_pairs={{0,2},{1,3},{2,0},{3,1},{4,6},{5,7},{6,4},{7,5},{8,10},{9,11},{10,... | collective-permute-start | bytes 3981320 | tf_op jit(solution)/shard_map/ppermute | solution.py:563
  84.4 31.5 %collective-permute-start.19 = (bf16[4,48,3456]{2,1,0:T(8,128)(2,1)S(1)}, bf16[4,48,3456]{2,1,0:T(8,128)(2,1)}, u32[]{:S(2)}, u32[]{:S(2)}) collective-permute-start(bf16[4,48,3456]{2,1,0:T(8,128)(2,1)S(1)} %constant_dynamic-update-slice_fusion.8.refs_0_), channel_id=1, source_target_pairs={{0,1},{1,0},{2,3},{3,2},{4,5},{5,4},{6,7},{7,6},{8,9},{9,8},{10,11... | collective-permute-start | bytes 3981320 | tf_op jit(solution)/shard_map/ppermute | solution.py:563
  84.4 31.5 %collective-permute-start.20 = (bf16[4,48,3456]{2,1,0:T(8,128)(2,1)S(1)}, bf16[4,48,3456]{2,1,0:T(8,128)(2,1)}, u32[]{:S(2)}, u32[]{:S(2)}) collective-permute-start(bf16[4,48,3456]{2,1,0:T(8,128)(2,1)S(1)} %constant_dynamic-update-slice_fusion.10.refs_1_), channel_id=1, source_target_pairs={{0,1},{1,0},{2,3},{3,2},{4,5},{5,4},{6,7},{7,6},{8,9},{9,8},{10,11... | collective-permute-start | bytes 3981320 | tf_op jit(solution)/shard_map/ppermute | solution.py:563
  178.8 16.4 %collective-permute-start.23 = (bf16[16,48,3456]{2,1,0:T(8,128)(2,1)}, bf16[16,48,3456]{2,1,0:T(8,128)(2,1)}, u32[]{:S(2)}, u32[]{:S(2)}) collective-permute-start(bf16[16,48,3456]{2,1,0:T(8,128)(2,1)} %get-tuple-element.67), channel_id=1, source_target_pairs={{0,1},{1,0},{2,3},{3,2},{4,5},{5,4},{6,7},{7,6},{8,9},{9,8},{10,11... | collective-permute-start | bytes 15925256 | tf_op jit(solution)/shard_map/ppermute | solution.py:563
  200.6 35.4 %collective-permute-start.33 = (bf16[2,2,48,3456]{3,2,0,1:T(8,128)(2,1)}, bf16[2,2,48,3456]{3,2,0,1:T(8,128)(2,1)}, u32[]{:S(2)}, u32[]{:S(2)}) collective-permute-start(bf16[2,2,48,3456]{3,2,0,1:T(8,128)(2,1)} %fusion), channel_id=1, source_target_pairs={{0,4},{1,5},{2,6},{3,7},{4,0},{5,1},{6,2},{7,3},{8,12},{9,13},{10,... | collective-permute-start | bytes 3981320 | tf_op jit(solution)/shard_map/ppermute | solution.py:563
  201.7 34.3 %collective-permute-start.34 = (bf16[2,2,48,3456]{3,2,0,1:T(8,128)(2,1)}, bf16[2,2,48,3456]{3,2,0,1:T(8,128)(2,1)S(1)}, u32[]{:S(2)}, u32[]{:S(2)}) collective-permute-start(bf16[2,2,48,3456]{3,2,0,1:T(8,128)(2,1)} %fusion.1), channel_id=1, source_target_pairs={{0,2},{1,3},{2,0},{3,1},{4,6},{5,7},{6,4},{7,5},{8,10},{9,11},{10,... | collective-permute-start | bytes 3981320 | tf_op jit(solution)/shard_map/ppermute | solution.py:563
  226.5 12.8 %collective-permute-start.24 = (bf16[16,48,1280]{2,1,0:T(8,128)(2,1)}, bf16[16,48,1280]{2,1,0:T(8,128)(2,1)S(1)}, u32[]{:S(2)}, u32[]{:S(2)}) collective-permute-start(bf16[16,48,1280]{2,1,0:T(8,128)(2,1)} %get-tuple-element.72), channel_id=1, source_target_pairs={{0,1},{1,0},{2,3},{3,2},{4,5},{5,4},{6,7},{7,6},{8,9},{9,8},{10,11... | collective-permute-start | bytes 5898248 | tf_op jit(solution)/shard_map/ppermute | solution.py:563
  237.7 17.8 %collective-permute-start.37 = (bf16[2,48,3456]{2,1,0:T(8,128)(2,1)S(1)}, bf16[2,48,3456]{2,1,0:T(8,128)(2,1)S(1)}, u32[]{:S(2)}, u32[]{:S(2)}) collective-permute-start(bf16[2,48,3456]{2,1,0:T(8,128)(2,1)S(1)} %fusion.2), channel_id=1, source_target_pairs={{0,4},{1,5},{2,6},{3,7},{4,0},{5,1},{6,2},{7,3},{8,12},{9,13},{10,... | collective-permute-start | bytes 1990664 | tf_op jit(solution)/shard_map/ppermute | solution.py:563
  239.4 25.3 %collective-permute-start.28 = (bf16[2,2,48,1280]{3,2,0,1:T(8,128)(2,1)S(1)}, bf16[2,2,48,1280]{3,2,0,1:T(8,128)(2,1)S(1)}, u32[]{:S(2)}, u32[]{:S(2)}) collective-permute-start(bf16[2,2,48,1280]{3,2,0,1:T(8,128)(2,1)S(1)} %fusion.11), channel_id=1, source_target_pairs={{0,2},{1,3},{2,0},{3,1},{4,6},{5,7},{6,4},{7,5},{8,10},{9,11},{10,... | collective-permute-start | bytes 1474568 | tf_op jit(solution)/shard_map/ppermute | solution.py:563
  240.2 40.0 %collective-permute-start.25 = (bf16[2,2,48,1280]{3,2,0,1:T(8,128)(2,1)S(1)}, bf16[2,2,48,1280]{3,2,0,1:T(8,128)(2,1)S(1)}, u32[]{:S(2)}, u32[]{:S(2)}) collective-permute-start(bf16[2,2,48,1280]{3,2,0,1:T(8,128)(2,1)S(1)} %fusion.10), channel_id=1, source_target_pairs={{0,4},{1,5},{2,6},{3,7},{4,0},{5,1},{6,2},{7,3},{8,12},{9,13},{10,... | collective-permute-start | bytes 1474568 | tf_op jit(solution)/shard_map/ppermute | solution.py:563
  257.9 16.1 %collective-permute-start.35 = (bf16[2,48,3456]{2,1,0:T(8,128)(2,1)S(1)}, bf16[2,48,3456]{2,1,0:T(8,128)(2,1)S(1)}, u32[]{:S(2)}, u32[]{:S(2)}) collective-permute-start(bf16[2,48,3456]{2,1,0:T(8,128)(2,1)S(1)} %get-tuple-element.86), channel_id=1, source_target_pairs={{0,2},{1,3},{2,0},{3,1},{4,6},{5,7},{6,4},{7,5},{8,10},{9,11},{10,... | collective-permute-start | bytes 1990664 | tf_op jit(solution)/shard_map/ppermute | solution.py:563
  259.2 28.1 %collective-permute-start.39 = (bf16[48,3456]{1,0:T(8,128)(2,1)S(1)}, bf16[48,3456]{1,0:T(8,128)(2,1)S(1)}, u32[]{:S(2)}, u32[]{:S(2)}) collective-permute-start(bf16[48,3456]{1,0:T(8,128)(2,1)S(1)} %get-tuple-element.92), channel_id=1, source_target_pairs={{0,24},{1,25},{2,26},{3,27},{4,28},{5,29},{6,30},{7,31},{8,16},{9,... | collective-permute-start | bytes 995336 | tf_op jit(solution)/shard_map/ppermute | solution.py:563
  261.7 34.8 %collective-permute-start.38 = (bf16[48,3456]{1,0:T(8,128)(2,1)S(1)}, bf16[48,3456]{1,0:T(8,128)(2,1)S(1)}, u32[]{:S(2)}, u32[]{:S(2)}) collective-permute-start(bf16[48,3456]{1,0:T(8,128)(2,1)S(1)} %get-tuple-element.91), channel_id=1, source_target_pairs={{0,16},{1,17},{2,18},{3,19},{4,20},{5,21},{6,22},{7,23},{8,24},{9,... | collective-permute-start | bytes 995336 | tf_op jit(solution)/shard_map/ppermute | solution.py:563
  264.8 15.4 %collective-permute-start.29 = (bf16[2,48,1280]{2,1,0:T(8,128)(2,1)S(1)}, bf16[2,48,1280]{2,1,0:T(8,128)(2,1)S(1)}, u32[]{:S(2)}, u32[]{:S(2)}) collective-permute-start(bf16[2,48,1280]{2,1,0:T(8,128)(2,1)S(1)} %fusion.12), channel_id=1, source_target_pairs={{0,4},{1,5},{2,6},{3,7},{4,0},{5,1},{6,2},{7,3},{8,12},{9,13},{10,... | collective-permute-start | bytes 737288 | tf_op jit(solution)/shard_map/ppermute | solution.py:563
  275.9 21.7 %collective-permute-start.36 = (bf16[48,3456]{1,0:T(8,128)(2,1)S(1)}, bf16[48,3456]{1,0:T(8,128)(2,1)S(1)}, u32[]{:S(2)}, u32[]{:S(2)}) collective-permute-start(bf16[48,3456]{1,0:T(8,128)(2,1)S(1)} %fusion.17), channel_id=1, source_target_pairs={{0,8},{1,9},{2,10},{3,11},{4,12},{5,13},{6,14},{7,15},{8,0},{9,1},... | collective-permute-start | bytes 995336 | tf_op jit(solution)/shard_map/ppermute | solution.py:563
  281.5 17.2 %collective-permute-start.31 = (bf16[48,1280]{1,0:T(8,128)(2,1)S(1)}, bf16[48,1280]{1,0:T(8,128)(2,1)S(1)}, u32[]{:S(2)}, u32[]{:S(2)}) collective-permute-start(bf16[48,1280]{1,0:T(8,128)(2,1)S(1)} %get-tuple-element.100), channel_id=1, source_target_pairs={{0,24},{1,25},{2,26},{3,27},{4,28},{5,29},{6,30},{7,31},{8,16},{9,... | collective-permute-start | bytes 368648 | tf_op jit(solution)/shard_map/ppermute | solution.py:563
  286.7 15.0 %collective-permute-start.30 = (bf16[48,1280]{1,0:T(8,128)(2,1)S(1)}, bf16[48,1280]{1,0:T(8,128)(2,1)S(1)}, u32[]{:S(2)}, u32[]{:S(2)}) collective-permute-start(bf16[48,1280]{1,0:T(8,128)(2,1)S(1)} %get-tuple-element.99), channel_id=1, source_target_pairs={{0,16},{1,17},{2,18},{3,19},{4,20},{5,21},{6,22},{7,23},{8,24},{9,... | collective-permute-start | bytes 368648 | tf_op jit(solution)/shard_map/ppermute | solution.py:563
  287.3 14.4 %collective-permute-start.27 = (bf16[48,1280]{1,0:T(8,128)(2,1)S(1)}, bf16[48,1280]{1,0:T(8,128)(2,1)S(1)}, u32[]{:S(2)}, u32[]{:S(2)}) collective-permute-start(bf16[48,1280]{1,0:T(8,128)(2,1)S(1)} %fusion.23), channel_id=1, source_target_pairs={{0,8},{1,9},{2,10},{3,11},{4,12},{5,13},{6,14},{7,15},{8,0},{9,1},... | collective-permute-start | bytes 368648 | tf_op jit(solution)/shard_map/ppermute | solution.py:563
  (22 other events, 208.2 us)
